TPU v7x, 32 devices: a whole 2x2x4 slice. The times are simulated.
32 devices in a mesh: video: 4 (over y, core), frame: 8 (over z, x).
Axes of the slice: x: 2, y: 2, z: 4, core: 2. Of those that a mesh axis runs over, the one named last changes fastest.
Arguments:
- hidden: bfloat16 [64, 256, 320], P(('video', 'frame')), parts along dimension 0, may hold values from -6 to 6
- ref_feats: bfloat16 [1024, 320], P(('video', 'frame')), parts along dimension 0, may hold values from -6 to 6
- frame_index: int32 [64], P(('video', 'frame')), parts along dimension 0, may hold values from 0 to 31
- step_index: int32 [1], replicated, may hold values from 0 to 999
- temb_table: bfloat16 [1000, 320], replicated, may hold values from -3 to 3
- norm_gain_1: float32 [320], replicated, may hold values from 0.1 to 1.9
- norm_gain_2: float32 [320], replicated, may hold values from 0.1 to 1.9
- sp_query: bfloat16 [320, 320], replicated, as said below
- sp_key: bfloat16 [320, 320], replicated, as said below
- sp_value: bfloat16 [320, 320], replicated, may hold values from -0.3125 to 0.3125
- sp_out: bfloat16 [320, 320], replicated, may hold values from -0.625 to 0.625
- tm_query: bfloat16 [320, 320], replicated, as said below
- tm_key: bfloat16 [320, 320], replicated, as said below
- tm_value: bfloat16 [320, 320], replicated, may hold values from -0.3125 to 0.3125
- tm_out: bfloat16 [320, 320], replicated, may hold values from -0.625 to 0.625
Outputs:
- mixed: bfloat16 [64, 256, 320], P(('video', 'frame')), parts along dimension 0
There are 4 independent parts, one for each index of `video`. A program takes and returns all parts, laid end to end along the dimension named above; an argument that names none is the same for every part. Nothing has to cross between parts.
Inputs may be any that keep to these rules, and one draw needn't show every extreme that they name: `sp_query`: a projection matrix. `sp_key`: a projection matrix. `tm_query`: a projection matrix. `tm_key`: a projection matrix.
All inputs are finite; a program needn't handle non-finite values.
Results may differ from a plain program's by a relative error of at most 0.015.
The roundings to bfloat16 on the way count: a program that leaves them out, or rounds other values in their place, can miss the bound.
Values may be sent and summed in bfloat16 or wider, within the bound.
A program may use at most 64 MiB of HBM per device.

v0:
```python
import math

import jax
import jax.numpy as jnp
from jax import lax
from jax.sharding import PartitionSpec as P

HEADS = 8


def layer_norm(values, gain):
    mean = jnp.mean(values, axis=-1, keepdims=True)
    centered = values - mean
    var = jnp.mean(centered * centered, axis=-1, keepdims=True)
    return centered * lax.rsqrt(var + 1e-05) * gain


def positional(frame_index, width):
    chan = jnp.arange(width)
    freq = jnp.exp(-(chan // 2 * 2).astype(jnp.float32) / width * math.log(10000.0))
    phase = (chan % 2).astype(jnp.float32) * (math.pi / 2)
    return jnp.sin(frame_index.astype(jnp.float32)[:, None] * freq[None, :] + phase[None, :])


def project(rows, weight):
    return jnp.dot(rows, weight, preferred_element_type=jnp.float32).astype(jnp.bfloat16)


def temporal_attend(query, keys, values):
    frames, count, width = query.shape
    head_dim = width // HEADS
    q = query.reshape(frames, count, HEADS, head_dim)
    k = keys.reshape(frames, count, HEADS, head_dim)
    v = values.reshape(frames, count, HEADS, head_dim)
    scores = jnp.einsum("fnhd,gnhd->nhfg", q, k, preferred_element_type=jnp.float32) / math.sqrt(
        head_dim
    )
    probs = jax.nn.softmax(scores, axis=-1).astype(jnp.bfloat16)
    out = jnp.einsum("nhfg,gnhd->fnhd", probs, v, preferred_element_type=jnp.float32)
    return out.astype(jnp.bfloat16).reshape(frames, count, width)


def flatten_block(block):
    return block.reshape(block.shape[0], block.shape[2], block.shape[3])


def on_device(
    hidden,
    ref_feats,
    frame_index,
    step_index,
    temb_table,
    norm_gain_1,
    norm_gain_2,
    sp_query,
    sp_key,
    sp_value,
    sp_out,
    tm_query,
    tm_key,
    tm_value,
    tm_out,
):
    frames_here, positions, width = hidden.shape
    head_dim = width // HEADS
    blocks = lax.axis_size("frame")
    share = positions // blocks
    temb = lax.dynamic_slice_in_dim(temb_table, step_index[0], 1, 0).astype(jnp.float32)
    base = hidden.astype(jnp.float32) + temb[None, :, :]
    normed_1 = layer_norm(base, norm_gain_1).astype(jnp.bfloat16)
    ref_local = layer_norm(ref_feats.astype(jnp.float32), norm_gain_1).astype(jnp.bfloat16)
    ref_all = lax.all_gather(ref_local, "frame", axis=0, tiled=True)
    ref_k = project(ref_all, sp_key)
    ref_v = project(ref_all, sp_value)
    q1 = project(normed_1, sp_query).reshape(frames_here, positions, HEADS, head_dim)
    k1 = project(normed_1, sp_key).reshape(frames_here, positions, HEADS, head_dim)
    v1 = project(normed_1, sp_value).reshape(frames_here, positions, HEADS, head_dim)
    ref_kh = ref_k.reshape(positions, HEADS, head_dim)
    ref_vh = ref_v.reshape(positions, HEADS, head_dim)
    scale = 1.0 / math.sqrt(head_dim)
    self_scores = jnp.einsum("fqhd,fkhd->fhqk", q1, k1, preferred_element_type=jnp.float32) * scale
    ref_scores = (
        jnp.einsum("fqhd,khd->fhqk", q1, ref_kh, preferred_element_type=jnp.float32) * scale
    )
    top = jnp.maximum(
        jnp.max(self_scores, axis=-1, keepdims=True), jnp.max(ref_scores, axis=-1, keepdims=True)
    )
    self_exp = jnp.exp(self_scores - top)
    ref_exp = jnp.exp(ref_scores - top)
    total = jnp.sum(self_exp, axis=-1, keepdims=True) + jnp.sum(ref_exp, axis=-1, keepdims=True)
    self_probs = (self_exp / total).astype(jnp.bfloat16)
    ref_probs = (ref_exp / total).astype(jnp.bfloat16)
    attn_1 = jnp.einsum("fhqk,fkhd->fqhd", self_probs, v1, preferred_element_type=jnp.float32)
    attn_1 = attn_1 + jnp.einsum(
        "fhqk,khd->fqhd", ref_probs, ref_vh, preferred_element_type=jnp.float32
    )
    attn_1 = attn_1.astype(jnp.bfloat16).reshape(frames_here, positions, width)
    mid = base + jnp.dot(attn_1, sp_out, preferred_element_type=jnp.float32)
    encoding = positional(frame_index, width)
    normed_2 = (layer_norm(mid, norm_gain_2) + encoding[:, None, :]).astype(jnp.bfloat16)
    moved = (
        project(normed_2, tm_query).reshape(frames_here, blocks, share, width),
        project(normed_2, tm_key).reshape(frames_here, blocks, share, width),
        project(normed_2, tm_value).reshape(frames_here, blocks, share, width),
    )
    result = temporal_attend(
        flatten_block(lax.all_to_all(moved[0], "frame", split_axis=1, concat_axis=0, tiled=True)),
        flatten_block(lax.all_to_all(moved[1], "frame", split_axis=1, concat_axis=0, tiled=True)),
        flatten_block(lax.all_to_all(moved[2], "frame", split_axis=1, concat_axis=0, tiled=True)),
    )
    attn_2 = result.reshape(result.shape[0], 1, result.shape[1], result.shape[2])
    returned = lax.all_to_all(attn_2, "frame", split_axis=0, concat_axis=1, tiled=True).reshape(
        frames_here, positions, width
    )
    return (mid + jnp.dot(returned, tm_out, preferred_element_type=jnp.float32)).astype(
        jnp.bfloat16
    )


def solution(mesh):
    in_specs = (
        P(("video", "frame"), None, None),
        P(("video", "frame"), None),
        P(("video", "frame")),
        P(),
        P(),
        P(),
        P(),
        P(),
        P(),
        P(),
        P(),
        P(),
        P(),
        P(),
        P(),
    )
    out_specs = P(("video", "frame"), None, None)
    return jax.shard_map(
        on_device, mesh=mesh, in_specs=in_specs, out_specs=out_specs, check_vma=False
    )
```

profile of v0, /device:TPU:0, one launch (start us, length us, event | category | flops | bytes accessed | tf_op | source)
XLA Modules:
  0.0 121.3 jit_solution(15537504921892357004)
XLA Ops:
  0.0 0.0 copy-start
  0.7 1.1 convert_reduce_fusion
  1.8 1.1 fusion.20
  3.0 1.2 multiply_reduce_fusion.3
  4.1 0.8 convert_reduce_fusion.1
  5.0 0.9 fusion.31
  5.9 0.8 fusion.33
  6.8 32.4 %all_gather.3 = bf16[256,320]{1,0:T(8,128)(2,1)S(1)} all-gather(bf16[32,320]{1,0:T(8,128)(2,1)S(1)} %fusion.33), channel_id=1, replica_groups=mesh['video'=4,'frame'=8] {'frame'}, dimensions={0}, use_global_device_ids=true | all-gather | bytes 184320 | tf_op jit(solution)/shard_map/all_gather | solution.py:72
  39.2 0.0 copy-done
  39.2 1.5 %convolution_convert_fusion.4 = bf16[2,256,320]{1,2,0:T(8,128)(2,1)S(1)} fusion(bf16[320,320]{1,0:T(8,128)(2,1)S(1)} %copy-done, bf16[2,256,320]{1,2,0:T(8,128)(2,1)} %param.15, f32[320]{0:T(512)} %param.20, f32[2,256]{1,0:T(2,128)S(1)} %add_rsqrt_fusion.1, f32[2,256]{1,0:T(2,128)S(1)} %broadcast_multiply_fusion.1, f32[320]{0:T(512)S(1)} %convert_reduce_fusion), kind=kOutput, calls=%fused_computation.28 | convolution fusion | flops 106004480 | bytes 866816 | tf_op jit(solution)/shard_map/dot_general | solution.py:26
  40.7 0.3 convolution_convert_fusion.8
  41.0 1.2 %convolution_convert_fusion.7 = bf16[256,320]{0,1:T(8,128)(2,1)S(1)} fusion(bf16[256,320]{1,0:T(8,128)(2,1)S(1)} %all_gather.3, bf16[320,320]{1,0:T(8,128)(2,1)} %param.24), kind=kOutput, calls=%fused_computation.31 | convolution fusion | flops 52510720 | bytes 532480 | tf_op jit(solution)/shard_map/dot_general | solution.py:26
  42.2 1.6 %convolution_convert_fusion.6 = bf16[2,256,320]{1,2,0:T(8,128)(2,1)S(1)} fusion(bf16[320,320]{1,0:T(8,128)(2,1)} %param.24, bf16[2,256,320]{1,2,0:T(8,128)(2,1)} %param.15, f32[320]{0:T(512)} %param.20, f32[2,256]{1,0:T(2,128)S(1)} %add_rsqrt_fusion.1, f32[2,256]{1,0:T(2,128)S(1)} %broadcast_multiply_fusion.1, f32[320]{0:T(512)S(1)} %convert_reduce_fusion), kind=kOutput, calls=%fused_computation.30 | convolution fusion | flops 106004480 | bytes 866816 | tf_op jit(solution)/shard_map/dot_general | solution.py:26
  43.8 0.0 copy-done.1
  43.8 0.0 copy-done.9
  43.8 0.0 copy-done.10
  43.8 0.5 convolution_convert_fusion.5
  44.4 0.8 multiply_reduce_fusion
  45.1 0.8 bitcast_reduce_fusion
  45.9 1.4 %fusion.3 = (f32[2,8,256]{2,1,0:T(8,128)S(1)}, f32[2,8,256]{2,1,0:T(8,128)S(1)}) fusion(f32[8,256,2,256]{3,1,0,2:T(8,128)S(1)} %get-tuple-element.10, f32[2,8,256]{2,1,0:T(8,128)S(1)} %max.10, f32[2,8,256,256]{2,3,1,0:T(8,128)S(1)} %get-tuple-element.8), kind=kLoop, calls=%fused_computation.9 | loop fusion | flops 6283264 | bytes 8437760 | tf_op jit(solution)/shard_map/reduce_sum | solution.py:90
  47.4 0.9 fusion.8
  48.3 0.0 copy-start.4
  48.3 0.0 copy-start.11
  48.3 0.0 copy-start.8
  48.3 0.0 copy-start.5
  48.4 0.9 fusion.11
  49.3 0.0 copy-start.6
  49.3 0.0 copy-done.4
  49.3 0.4 fusion.63
  49.7 0.0 copy-start.7
  49.7 0.1 multiply_reduce_fusion.2
  49.8 0.0 copy-done.11
  49.9 0.1 add_sine_fusion
  50.0 0.0 copy-done.8
  50.0 0.2 add_convert_fusion
  50.2 0.0 copy-done.5
  50.2 0.4 convolution_convert_fusion.2
  50.6 0.2 copy.68
  50.8 0.8 copy.69
  51.6 5.5 %all-to-all-start.1 = ((bf16[2,8,32,320]{3,2,0,1:T(8,128)(2,1)}), bf16[2,8,32,320]{3,2,0,1:T(8,128)(2,1)S(1)}, u32[]{:S(2)}, u32[]{:S(2)}) async-start(bf16[2,8,32,320]{3,2,0,1:T(8,128)(2,1)} %copy.69), calls=%async_computation.1 | async-start | bytes 786432 | tf_op jit(solution)/shard_map/all_to_all | solution.py:107
  57.1 0.0 copy-done.6
  57.1 0.4 convolution_convert_fusion.1
  57.5 0.2 copy.71
  57.7 0.8 copy.72
  58.5 7.9 %all-to-all-done.1 = bf16[2,8,32,320]{3,2,0,1:T(8,128)(2,1)S(1)} async-done(((bf16[2,8,32,320]{3,2,0,1:T(8,128)(2,1)}), bf16[2,8,32,320]{3,2,0,1:T(8,128)(2,1)S(1)}, u32[]{:S(2)}, u32[]{:S(2)}) %all-to-all-start.1) | async-done | bytes 327712 | tf_op jit(solution)/shard_map/all_to_all | solution.py:107
  66.4 5.4 %all-to-all-start.2 = ((bf16[2,8,32,320]{3,2,0,1:T(8,128)(2,1)}), bf16[2,8,32,320]{3,2,0,1:T(8,128)(2,1)S(1)}, u32[]{:S(2)}, u32[]{:S(2)}) async-start(bf16[2,8,32,320]{3,2,0,1:T(8,128)(2,1)} %copy.72), calls=%async_computation.2 | async-start | bytes 786432 | tf_op jit(solution)/shard_map/all_to_all | solution.py:108
  71.8 0.4 convolution_convert_fusion.3
  72.2 0.2 copy.65
  72.4 0.8 copy.66
  73.2 11.0 %all-to-all-done.2 = bf16[2,8,32,320]{3,2,0,1:T(8,128)(2,1)S(1)} async-done(((bf16[2,8,32,320]{3,2,0,1:T(8,128)(2,1)}), bf16[2,8,32,320]{3,2,0,1:T(8,128)(2,1)S(1)}, u32[]{:S(2)}, u32[]{:S(2)}) %all-to-all-start.2) | async-done | bytes 327712 | tf_op jit(solution)/shard_map/all_to_all | solution.py:108
  84.3 4.2 %all-to-all-start = ((bf16[2,8,32,320]{3,2,0,1:T(8,128)(2,1)}), bf16[2,8,32,320]{3,2,0,1:T(8,128)(2,1)S(1)}, u32[]{:S(2)}, u32[]{:S(2)}) async-start(bf16[2,8,32,320]{3,2,0,1:T(8,128)(2,1)} %copy.66), calls=%async_computation | async-start | bytes 786432 | tf_op jit(solution)/shard_map/all_to_all | solution.py:109
  88.5 0.9 reshape_reshape.13
  89.3 1.8 %reshape_reshape.14 = bf16[16,32,8,40]{3,2,1,0:T(8,128)(2,1)} reshape(bf16[8,2,1,32,320]{4,3,1,0,2:T(8,128)(2,1)S(1)} %bitcast.110) | data formatting | bytes 655360 | tf_op jit(solution)/shard_map/reshape;reshape | solution.py:33
  91.2 6.5 %all-to-all-done = bf16[2,8,32,320]{3,2,0,1:T(8,128)(2,1)S(1)} async-done(((bf16[2,8,32,320]{3,2,0,1:T(8,128)(2,1)}), bf16[2,8,32,320]{3,2,0,1:T(8,128)(2,1)S(1)}, u32[]{:S(2)}, u32[]{:S(2)}) %all-to-all-start) | async-done | bytes 327712 | tf_op jit(solution)/shard_map/all_to_all | solution.py:109
  97.7 1.8 %reshape_reshape.12 = bf16[16,32,8,40]{3,2,1,0:T(8,128)(2,1)} reshape(bf16[8,2,1,32,320]{4,3,1,0,2:T(8,128)(2,1)S(1)} %bitcast.111) | data formatting | bytes 655360 | tf_op jit(solution)/shard_map/reshape;reshape | solution.py:34
  99.5 4.6 %fusion.64 = (f32[32,8,16]{2,1,0:T(8,128)S(1)}, f32[32,8,16,16]{2,3,1,0:T(8,128)}) fusion(bf16[16,32,8,40]{3,2,1,0:T(8,128)(2,1)} %reshape_reshape.14, bf16[16,32,8,40]{3,2,1,0:T(8,128)(2,1)S(1)} %reshape_reshape.13), kind=kOutput, calls=%fused_computation.91 | convolution fusion | flops 5439503 | bytes 933888 | tf_op jit(solution)/shard_map/sub | solution.py:38
  104.1 0.0 copy-done.2
  104.1 2.5 %fusion.7 = bf16[16,32,8,40]{3,0,2,1:T(8,128)(2,1)S(1)} fusion(f32[32,8,16,16]{2,3,1,0:T(8,128)} %get-tuple-element.14, bf16[16,32,8,40]{3,2,1,0:T(8,128)(2,1)S(1)} %copy-done.2, f32[32,8,16]{2,1,0:T(8,128)S(1)} %get-tuple-element.13), kind=kOutput, calls=%fused_computation.17 | convolution fusion | flops 5537792 | bytes 933888 | tf_op jit(solution)/shard_map/nhfg,gnhd->fnhd/dot_general | solution.py:39
  106.6 0.0 copy-start.3
  106.6 0.3 copy.77
  106.9 0.7 reshape_reshape.15
  107.6 12.6 %all_to_all.60 = bf16[16,1,32,320]{3,2,1,0:T(8,128)(2,1)S(1)} all-to-all(bf16[16,1,32,320]{3,2,1,0:T(8,128)(2,1)S(1)} %bitcast.116), channel_id=1, replica_groups=mesh['video'=4,'frame'=8] {'frame'}, dimensions={0} | all-to-all | bytes 655360 | tf_op jit(solution)/shard_map/all_to_all | solution.py:112
  120.2 0.0 copy-done.3
  120.2 1.1 fusion.12
  (16 shorter events, 0.1 us)
Async XLA Ops:
  0.0 39.2 %copy-start = (bf16[320,320]{1,0:T(8,128)(2,1)S(1)}, bf16[320,320]{1,0:T(8,128)(2,1)}, u32[]{:S(2)}) copy-start(bf16[320,320]{1,0:T(8,128)(2,1)} %param.23) | copy-start | bytes 614404
  0.0 43.8 %copy-start.1 = (bf16[2,256,320]{1,2,0:T(8,128)(2,1)S(1)}, bf16[2,256,320]{1,2,0:T(8,128)(2,1)}, u32[]{:S(2)}) copy-start(bf16[2,256,320]{1,2,0:T(8,128)(2,1)} %param.15) | copy-start | bytes 983044
  0.0 43.8 %copy-start.9 = (f32[320]{0:T(512)S(1)}, f32[320]{0:T(512)}, u32[]{:S(2)}) copy-start(f32[320]{0:T(512)} %param.20) | copy-start | bytes 3844
  0.0 43.8 %copy-start.10 = (bf16[320,320]{1,0:T(8,128)(2,1)S(1)}, bf16[320,320]{1,0:T(8,128)(2,1)}, u32[]{:S(2)}) copy-start(bf16[320,320]{1,0:T(8,128)(2,1)} %param.22) | copy-start | bytes 614404
  48.3 1.0 copy-start.4
  48.3 1.5 %copy-start.11 = (s32[2]{0:T(128)S(1)}, s32[2]{0:T(128)}, u32[]{:S(2)}) copy-start(s32[2]{0:T(128)} %param.17) | copy-start | bytes 28
  48.3 1.7 %copy-start.8 = (f32[320]{0:T(512)S(1)}, f32[320]{0:T(512)}, u32[]{:S(2)}) copy-start(f32[320]{0:T(512)} %param.21) | copy-start | bytes 3844
  48.3 1.9 %copy-start.5 = (bf16[320,320]{1,0:T(8,128)(2,1)S(1)}, bf16[320,320]{1,0:T(8,128)(2,1)}, u32[]{:S(2)}) copy-start(bf16[320,320]{1,0:T(8,128)(2,1)} %param.26) | copy-start | bytes 614404
  49.3 7.8 %copy-start.6 = (bf16[320,320]{1,0:T(8,128)(2,1)S(1)}, bf16[320,320]{1,0:T(8,128)(2,1)}, u32[]{:S(2)}) copy-start(bf16[320,320]{1,0:T(8,128)(2,1)} %param.27) | copy-start | bytes 614404
  49.7 22.1 %copy-start.7 = (bf16[320,320]{1,0:T(8,128)(2,1)S(1)}, bf16[320,320]{1,0:T(8,128)(2,1)}, u32[]{:S(2)}) copy-start(bf16[320,320]{1,0:T(8,128)(2,1)} %param.28) | copy-start | bytes 614404
  51.6 14.8 %all-to-all-start.1 = ((bf16[2,8,32,320]{3,2,0,1:T(8,128)(2,1)}), bf16[2,8,32,320]{3,2,0,1:T(8,128)(2,1)S(1)}, u32[]{:S(2)}, u32[]{:S(2)}) async-start(bf16[2,8,32,320]{3,2,0,1:T(8,128)(2,1)} %copy.69), calls=%async_computation.1 | async-start | bytes 786432 | tf_op jit(solution)/shard_map/all_to_all | solution.py:107
  66.4 17.9 %all-to-all-start.2 = ((bf16[2,8,32,320]{3,2,0,1:T(8,128)(2,1)}), bf16[2,8,32,320]{3,2,0,1:T(8,128)(2,1)S(1)}, u32[]{:S(2)}, u32[]{:S(2)}) async-start(bf16[2,8,32,320]{3,2,0,1:T(8,128)(2,1)} %copy.72), calls=%async_computation.2 | async-start | bytes 786432 | tf_op jit(solution)/shard_map/all_to_all | solution.py:108
  84.3 13.4 %all-to-all-start = ((bf16[2,8,32,320]{3,2,0,1:T(8,128)(2,1)}), bf16[2,8,32,320]{3,2,0,1:T(8,128)(2,1)S(1)}, u32[]{:S(2)}, u32[]{:S(2)}) async-start(bf16[2,8,32,320]{3,2,0,1:T(8,128)(2,1)} %copy.66), calls=%async_computation | async-start | bytes 786432 | tf_op jit(solution)/shard_map/all_to_all | solution.py:109
  99.5 4.6 %copy-start.2 = (bf16[16,32,8,40]{3,2,1,0:T(8,128)(2,1)S(1)}, bf16[16,32,8,40]{3,2,1,0:T(8,128)(2,1)}, u32[]{:S(2)}) copy-start(bf16[16,32,8,40]{3,2,1,0:T(8,128)(2,1)} %reshape_reshape.12) | copy-start | bytes 983044
  106.6 13.7 %copy-start.3 = (bf16[320,320]{1,0:T(8,128)(2,1)S(1)}, bf16[320,320]{1,0:T(8,128)(2,1)}, u32[]{:S(2)}) copy-start(bf16[320,320]{1,0:T(8,128)(2,1)} %param.29) | copy-start | bytes 614404
where the time goes:
time: 122 us; the launch traced here: 121 us
  blocking collectives  45 us (37%)
  waiting for transfers between devices  25.4 us (21%)
  matrix products  18.2 us (15%)
  starting transfers between devices  15.1 us (12%)
  local copies, waits for them, and re-layouts  8.64 us (7%)
  other arithmetic  7.85 us (6%)
    all_gather x1, blocking collectives, on_device(): ref_all = lax.all_gather(ref_local, 'frame', axis=0, tiled=True)  32.4 us
    all_to_all x1, blocking collectives, on_device(): lax.all_to_all(attn_2, 'frame', split_axis=0, concat_axis=1, tiled=True)  12.6 us
    all_to_all x1, waiting for transfers between devices, on_device(): lax.all_to_all(moved[1], 'frame', split_axis=1, concat_axis=0, tiled=True)  11 us
    all_to_all x1, waiting for transfers between devices, on_device(): lax.all_to_all(moved[0], 'frame', split_axis=1, concat_axis=0, tiled=True)  7.89 us
    all_to_all x1, waiting for transfers between devices, on_device(): lax.all_to_all(moved[2], 'frame', split_axis=1, concat_axis=0, tiled=True)  6.49 us
    dot_general x8, matrix products, project(): jnp.dot(rows, weight, preferred_element_type=jnp.float32)  6.23 us
    all_to_all x1, starting transfers between devices, on_device(): lax.all_to_all(moved[0], 'frame', split_axis=1, concat_axis=0, tiled=True)  5.49 us
    all_to_all x1, starting transfers between devices, on_device(): lax.all_to_all(moved[1], 'frame', split_axis=1, concat_axis=0, tiled=True)  5.42 us
  transfers between devices with their start and end apart: 3, of which 3 were waited for; matrix products, arithmetic and copies ran while one was open for 5% of the time, Pallas kernels for 0%

commit v1 on v0

--- a/solution.py
+++ b/solution.py
@@ -1,8 +1,11 @@
+import functools
 import math
 
 import jax
 import jax.numpy as jnp
 from jax import lax
+from jax.experimental import pallas as pl
+from jax.experimental.pallas import tpu as pltpu
 from jax.sharding import PartitionSpec as P
 
 HEADS = 8
@@ -44,7 +47,7 @@
     return block.reshape(block.shape[0], block.shape[2], block.shape[3])
 
 
-def on_device(
+def on_device_plain(
     hidden,
     ref_feats,
     frame_index,
@@ -117,6 +120,329 @@
     )
 
 
+def head_span(head, head_dim, width):
+    low = head * head_dim
+    high = low + head_dim
+    return low, high, low // 128 * 128, min(width, -(-high // 128) * 128)
+
+
+def lane_mask(low, high, first, last):
+    lane = lax.broadcasted_iota(jnp.int32, (1, last - first), 1) + first
+    return jnp.where((lane >= low) & (lane < high), 1.0, 0.0).astype(jnp.bfloat16)
+
+
+def attend_heads(q, key_parts, value_parts, width, allowed=None):
+    head_dim = width // HEADS
+    factor = math.log2(math.e) / math.sqrt(head_dim)
+    columns = [None] * (-(-width // 128))
+    for head in range(HEADS):
+        low, high, first, last = head_span(head, head_dim, width)
+        picked = q[:, first:last] * lane_mask(low, high, first, last)
+        scores = [
+            lax.dot_general(
+                picked,
+                keys(first, last),
+                (((1,), (1,)), ((), ())),
+                preferred_element_type=jnp.float32,
+            )
+            for keys in key_parts
+        ]
+        if allowed is not None:
+            scores = [jnp.where(allowed, s, -1e30) for s in scores]
+        top = functools.reduce(jnp.maximum, [jnp.max(s, axis=-1, keepdims=True) for s in scores])
+        exps = [jnp.exp2((s - top) * factor) for s in scores]
+        total = sum(jnp.sum(e, axis=-1, keepdims=True) for e in exps)
+        inverse = 1.0 / total
+        result = None
+        for e, values in zip(exps, value_parts):
+            probs = (e * inverse).astype(jnp.bfloat16)
+            part = jnp.dot(probs, values(first, last), preferred_element_type=jnp.float32)
+            result = part if result is None else result + part
+        for block in range(first // 128, -(-last // 128)):
+            start, end = block * 128, min(width, block * 128 + 128)
+            piece = result[:, start - first : end - first]
+            if columns[block] is not None:
+                lane = lax.broadcasted_iota(jnp.int32, (1, end - start), 1) + start
+                piece = jnp.where(lane >= low, piece, columns[block])
+            columns[block] = piece
+    return jnp.concatenate(columns, axis=-1)
+
+
+def fused_kernel(
+    blocks,
+    step_ref,
+    frame_ref,
+    hidden_ref,
+    ref_ref,
+    temb_ref,
+    gain1_ref,
+    gain2_ref,
+    spq_ref,
+    spk_ref,
+    spv_ref,
+    spo_ref,
+    tmq_ref,
+    tmk_ref,
+    tmv_ref,
+    tmo_ref,
+    out_ref,
+    ref_buf,
+    q_buf,
+    k_buf,
+    v_buf,
+    rk_buf,
+    rv_buf,
+    mid_buf,
+    pe_buf,
+    fwd_out,
+    fwd_in,
+    bwd_out,
+    bwd_in,
+    ref_send,
+    ref_recv,
+    fwd_send,
+    fwd_recv,
+    bwd_send,
+    bwd_recv,
+):
+    me = lax.axis_index("frame")
+    frames_here, _, halves, rows, width = hidden_ref.shape
+    count = blocks * rows
+    frames = frames_here * blocks
+    bf16 = jnp.bfloat16
+
+    def peer(shift):
+        return lax.rem(me + shift, blocks)
+
+    barrier = pltpu.get_barrier_semaphore()
+    for shift in range(1, blocks):
+        pl.semaphore_signal(
+            barrier, inc=1, device_id={"frame": peer(shift)}, device_id_type=pl.DeviceIdType.MESH
+        )
+
+    gain1 = gain1_ref[...]
+    ref_buf[me] = layer_norm(ref_ref[...].astype(jnp.float32), gain1).astype(bf16)
+    pl.semaphore_wait(barrier, blocks - 1)
+
+    def ref_copy(shift):
+        return pltpu.make_async_remote_copy(
+            src_ref=ref_buf.at[me],
+            dst_ref=ref_buf.at[me],
+            send_sem=ref_send.at[shift - 1],
+            recv_sem=ref_recv.at[shift - 1],
+            device_id={"frame": peer(shift)},
+            device_id_type=pl.DeviceIdType.MESH,
+        )
+
+    def fwd_copy(half, shift):
+        return pltpu.make_async_remote_copy(
+            src_ref=fwd_out.at[half, peer(shift)],
+            dst_ref=fwd_in.at[half, me],
+            send_sem=fwd_send.at[half, shift - 1],
+            recv_sem=fwd_recv.at[half, shift - 1],
+            device_id={"frame": peer(shift)},
+            device_id_type=pl.DeviceIdType.MESH,
+        )
+
+    def bwd_copy(half, shift):
+        return pltpu.make_async_remote_copy(
+            src_ref=bwd_out.at[half, peer(shift)],
+            dst_ref=bwd_in.at[half, me],
+            send_sem=bwd_send.at[half, shift - 1],
+            recv_sem=bwd_recv.at[half, shift - 1],
+            device_id={"frame": peer(shift)},
+            device_id_type=pl.DeviceIdType.MESH,
+        )
+
+    for shift in range(1, blocks):
+        ref_copy(shift).start()
+
+    step = step_ref[0]
+    rows8 = temb_ref[step // 8].astype(jnp.float32)
+    row_id = lax.broadcasted_iota(jnp.int32, rows8.shape, 0)
+    temb = jnp.sum(jnp.where(row_id == step % 8, rows8, 0.0), axis=0, keepdims=True)
+
+    chan = lax.broadcasted_iota(jnp.int32, (1, width), 1)
+    freq = jnp.exp(-(chan // 2 * 2).astype(jnp.float32) / width * math.log(10000.0))
+    phase = (chan % 2).astype(jnp.float32) * (math.pi / 2)
+    for f in range(frames_here):
+        pe_buf[f] = jnp.sin(frame_ref[f].astype(jnp.float32) * freq + phase)
+
+    for f in range(frames_here):
+        normed = []
+        for half in range(halves):
+            base = hidden_ref[f, :, half].reshape(count, width).astype(jnp.float32) + temb
+            mid_buf[half, f] = base
+            normed.append(layer_norm(base, gain1).astype(bf16))
+        normed = jnp.concatenate(normed, axis=0)
+        query = project(normed, spq_ref[...])
+        for half in range(halves):
+            q_buf[half, f] = query[half * count : (half + 1) * count]
+        k_buf[f] = project(normed, spk_ref[...])
+        v_buf[f] = project(normed, spv_ref[...])
+
+    for shift in range(1, blocks):
+        ref_copy(shift).wait_recv()
+    ref_all = ref_buf[...].reshape(-1, width)
+    rk_buf[...] = project(ref_all, spk_ref[...])
+    rv_buf[...] = project(ref_all, spv_ref[...])
+
+    gain2 = gain2_ref[...]
+
+    def spatial(half, carry):
+        for f in range(frames_here):
+            attn = attend_heads(
+                q_buf[half, f],
+                [lambda a, b: k_buf[f, :, a:b], lambda a, b: rk_buf[:, a:b]],
+                [lambda a, b: v_buf[f, :, a:b], lambda a, b: rv_buf[:, a:b]],
+                width,
+            ).astype(bf16)
+            mid = mid_buf[half, f] + jnp.dot(
+                attn, spo_ref[...], preferred_element_type=jnp.float32
+            )
+            mid_buf[half, f] = mid
+            normed = (layer_norm(mid, gain2) + pe_buf[f]).astype(bf16)
+            fwd_out[half, :, f] = normed.reshape(blocks, rows, width)
+        for shift in range(1, blocks):
+            fwd_copy(half, shift).start()
+        fwd_in[half, me] = fwd_out[half, me]
+        return carry
+
+    lax.fori_loop(0, halves, spatial, 0)
+
+    group = 8
+    size = frames * group
+    row_pos = lax.broadcasted_iota(jnp.int32, (size, size), 0) % group
+    col_pos = lax.broadcasted_iota(jnp.int32, (size, size), 1) % group
+    same = row_pos == col_pos
+
+    def temporal(half, carry):
+        for shift in range(1, blocks):
+            fwd_copy(half, shift).wait_recv()
+        normed = fwd_in[half].reshape(frames * rows, width)
+
+        def grouped(weight_ref):
+            full = jnp.dot(normed, weight_ref[...], preferred_element_type=jnp.float32)
+            full = full.reshape(frames, rows // group, group, width)
+            return [full[:, g].reshape(size, width).astype(bf16) for g in range(rows // group)]
+
+        q2, k2, v2 = grouped(tmq_ref), grouped(tmk_ref), grouped(tmv_ref)
+        done = []
+        for g in range(rows // group):
+            attn = attend_heads(
+                q2[g],
+                [lambda a, b: k2[g][:, a:b]],
+                [lambda a, b: v2[g][:, a:b]],
+                width,
+                same,
+            )
+            done.append(attn.reshape(frames, 1, group, width))
+        attn = jnp.concatenate(done, axis=1).reshape(blocks, frames_here, rows, width)
+        bwd_out[half] = attn.astype(bf16)
+        for shift in range(1, blocks):
+            bwd_copy(half, shift).start()
+        bwd_in[half, me] = bwd_out[half, me]
+        return carry
+
+    lax.fori_loop(0, halves, temporal, 0)
+
+    def finish(half, carry):
+        for shift in range(1, blocks):
+            bwd_copy(half, shift).wait_recv()
+        for f in range(frames_here):
+            attn = bwd_in[half, :, f].reshape(count, width)
+            mixed = mid_buf[half, f] + jnp.dot(
+                attn, tmo_ref[...], preferred_element_type=jnp.float32
+            )
+            out_ref[f, :, half] = mixed.astype(bf16).reshape(blocks, rows, width)
+        return carry
+
+    lax.fori_loop(0, halves, finish, 0)
+
+    for shift in range(1, blocks):
+        ref_copy(shift).wait_send()
+        for half in range(halves):
+            fwd_copy(half, shift).wait_send()
+            bwd_copy(half, shift).wait_send()
+
+
+def on_device_fused(
+    hidden,
+    ref_feats,
+    frame_index,
+    step_index,
+    temb_table,
+    norm_gain_1,
+    norm_gain_2,
+    *weights,
+):
+    frames_here, positions, width = hidden.shape
+    blocks = lax.axis_size("frame")
+    share = positions // blocks
+    halves = 2
+    rows = share // halves
+    count = blocks * rows
+    ref_rows = ref_feats.shape[0]
+    bf16 = jnp.bfloat16
+    dma = pltpu.SemaphoreType.DMA
+    smem = pl.BlockSpec(memory_space=pltpu.SMEM)
+    vmem = pl.BlockSpec(memory_space=pltpu.VMEM)
+    moved = (halves, blocks, frames_here, rows, width)
+    out = pl.pallas_call(
+        functools.partial(fused_kernel, blocks),
+        out_shape=jax.ShapeDtypeStruct((frames_here, blocks, halves, rows, width), bf16),
+        in_specs=[smem, smem] + [vmem] * 13,
+        out_specs=vmem,
+        scratch_shapes=[
+            pltpu.VMEM((blocks, ref_rows, width), bf16),
+            pltpu.VMEM((halves, frames_here, count, width), bf16),
+            pltpu.VMEM((frames_here, positions, width), bf16),
+            pltpu.VMEM((frames_here, positions, width), bf16),
+            pltpu.VMEM((blocks * ref_rows, width), bf16),
+            pltpu.VMEM((blocks * ref_rows, width), bf16),
+            pltpu.VMEM((halves, frames_here, count, width), jnp.float32),
+            pltpu.VMEM((frames_here, 1, width), jnp.float32),
+            pltpu.VMEM(moved, bf16),
+            pltpu.VMEM(moved, bf16),
+            pltpu.VMEM(moved, bf16),
+            pltpu.VMEM(moved, bf16),
+            dma((blocks - 1,)),
+            dma((blocks - 1,)),
+            dma((halves, blocks - 1)),
+            dma((halves, blocks - 1)),
+            dma((halves, blocks - 1)),
+            dma((halves, blocks - 1)),
+        ],
+        compiler_params=pltpu.CompilerParams(
+            collective_id=0, has_side_effects=True, vmem_limit_bytes=32 * 1024 * 1024
+        ),
+    )(
+        step_index,
+        frame_index,
+        hidden.reshape(frames_here, blocks, halves, rows, width),
+        ref_feats,
+        temb_table.reshape(-1, 8, width),
+        norm_gain_1.reshape(1, width),
+        norm_gain_2.reshape(1, width),
+        *weights,
+    )
+    return out.reshape(frames_here, positions, width)
+
+
+def on_device(hidden, ref_feats, frame_index, step_index, temb_table, *rest):
+    blocks = lax.axis_size("frame")
+    frames_here, positions, width = hidden.shape
+    fits = (
+        positions % (32 * blocks) == 0
+        and blocks * ref_feats.shape[0] == positions
+        and ref_feats.shape[0] % 16 == 0
+        and temb_table.shape[0] % 8 == 0
+        and frames_here * blocks * 8 <= 128
+    )
+    body = on_device_fused if fits else on_device_plain
+    return body(hidden, ref_feats, frame_index, step_index, temb_table, *rest)
+
+
 def solution(mesh):
     in_specs = (
         P(("video", "frame"), None, None),

time: 122 us -> 45.5 us (0.37)
  blocking collectives: 45 us -> 0 us
  Pallas kernels: 0 us -> 39.4 us
  waiting for transfers between devices: 25.4 us -> 0 us
  matrix products: 18.2 us -> 0 us
  starting transfers between devices: 15.1 us -> 0 us
  other arithmetic: 7.85 us -> 0 us
  local copies, waits for them, and re-layouts: 8.64 us -> 5.05 us
    pallas_call x0 -> x1, Pallas kernels: none -> 39.4 us  [on_device_fused(): pl.pallas_call(functools.partial(fused_kernel, blocks), out_shape=jax.Sha...]
    all_gather x1 -> x0, blocking collectives: 32.4 us -> none  [on_device(): ref_all = lax.all_gather(ref_local, 'frame', axis=0, tiled=True)]
    all_to_all x3 -> x0, waiting for transfers between devices: 25.4 us -> none  [the longest x1 11 us: on_device(): lax.all_to_all(moved[1], 'frame', split_axis=1, concat_axis=0, tiled=True)]
    all_to_all x3 -> x0, starting transfers between devices: 15.1 us -> none  [the longest x1 5.49 us: on_device(): lax.all_to_all(moved[0], 'frame', split_axis=1, concat_axis=0, tiled=True)]
    dot_general x15 -> x0, matrix products: 13.6 us -> none  [the longest x8 6.23 us: project(): jnp.dot(rows, weight, preferred_element_type=jnp.float32)]
    all_to_all x1 -> x0, blocking collectives: 12.6 us -> none  [on_device(): lax.all_to_all(attn_2, 'frame', split_axis=0, concat_axis=1, tiled=True)]
    reduce_sum x6 -> x0, other arithmetic: 5.57 us -> none  [the longest x3 2.17 us: layer_norm(): var = jnp.mean(centered * centered, axis=-1, keepdims=True)]
    another operation x4 -> x0, local copies, waits for them, and re-layouts: 5.25 us -> none  [the longest x1 1.85 us: temporal_attend(): k = keys.reshape(frames, count, HEADS, head_dim)]
  transfers between devices with their start and end apart: 3 -> 0, of which waited for: 3 -> 0; matrix products, arithmetic and copies ran while one was open for 5% -> 0% of each run, Pallas kernels for 0% -> 0%
where the time goes in v1:
time: 45.5 us; the launch traced here: 45.3 us
  Pallas kernels  39.4 us (87%)
  local copies, waits for them, and re-layouts  5.05 us (11%)
  between operations  0.82 us (2%)
    pallas_call x1, Pallas kernels, on_device_fused(): pl.pallas_call(functools.partial(fused_kernel, blocks), out_shape=jax.Sha...  39.4 us
    unnamed x24, local copies, waits for them, and re-layouts  3.45 us
    reshape x1, local copies, waits for them, and re-layouts, on_device_fused(): return out.reshape(frames_here, positions, width)  0.91 us

profile of v1, /device:TPU:0, one launch (start us, length us, event | category | flops | bytes accessed | tf_op | source)
XLA Modules:
  0.0 45.3 jit_solution(1391433887382173842)
XLA Ops:
  0.7 0.0 copy-start.10
  0.7 0.7 %reshape.17.gain1_ref = f32[1,320]{1,0:T(1,128)S(1)} reshape(f32[320]{0:T(512)} %param.20) | data formatting | bytes 2560 | tf_op jit(solution)/shard_map/reshape | solution.py:425
  1.4 0.0 copy-done.10
  1.4 0.0 copy-start.5
  1.4 0.0 copy-start.6
  1.4 0.0 copy-start.7
  1.4 1.3 %copy.16 = bf16[2,256,320]{2,1,0:T(8,128)(2,1)S(1)} copy(bf16[2,256,320]{1,2,0:T(8,128)(2,1)} %param.15) | data formatting | bytes 655360 | tf_op args[0]
  2.6 0.0 copy-start
  2.7 0.0 copy-start.1
  2.7 0.0 copy-start.2
  2.7 0.0 copy-start.3
  2.7 0.0 copy-start.4
  2.7 0.0 copy-start.8
  2.7 1.6 %copy.17 = bf16[1000,320]{1,0:T(8,128)(2,1)S(1)} copy(bf16[1000,320]{0,1:T(8,128)(2,1)} %param.19) | data formatting | bytes 1280000 | tf_op args[4]
  4.3 0.0 copy-start.9
  4.3 0.0 copy-done.5
  4.3 0.0 copy-done.6
  4.3 0.0 copy-done.7
  4.3 0.0 copy-done
  4.3 0.0 copy-done.1
  4.4 0.0 copy-done.2
  4.4 0.0 copy-done.3
  4.4 0.0 copy-done.4
  4.4 0.0 copy-done.8
  4.4 0.6 %copy-done.9 = s32[2]{0:T(128)S(1)} copy-done((s32[2]{0:T(128)S(1)}, s32[2]{0:T(128)}, u32[]{:S(2)}) %copy-start.9) | copy-done | bytes 32
  5.0 39.4 %shard_map.145 = bf16[2,8,2,16,320]{4,3,2,1,0:T(8,128)(2,1)S(1)} custom-call(s32[1]{0:T(128)S(6)} %copy.19.step_ref, s32[2]{0:T(128)S(1)} %copy-done.9, bf16[2,8,2,16,320]{4,3,2,1,0:T(8,128)(2,1)S(1)} %bitcast.5, bf16[32,320]{1,0:T(8,128)(2,1)S(1)} %copy-done.8, bf16[125,8,320]{2,1,0:T(8,128)(2,1)S(1)} %bitcast.3, f32[1,320]{1,0:T(1,128)S(1)} %reshape.17.gain1_ref, ...), custom_call_target="tpu_custom_call" | custom-call | tf_op jit(solution)/shard_map/pallas_call | solution.py:391
  44.4 0.9 %copy.18 = bf16[2,256,320]{1,2,0:T(8,128)(2,1)} copy(bf16[2,256,320]{2,1,0:T(8,128)(2,1)S(1)} %bitcast.4) | data formatting | bytes 655360 | tf_op jit(solution)/shard_map/reshape | solution.py:429
  (1 shorter events, 0.0 us)
Async XLA Ops:
  0.7 0.7 %copy-start.10 = (f32[320]{0:T(512)S(1)}, f32[320]{0:T(512)}, u32[]{:S(2)}) copy-start(f32[320]{0:T(512)} %param.21) | copy-start | bytes 3844
  1.4 2.9 %copy-start.5 = (bf16[320,320]{1,0:T(8,128)(2,1)S(1)}, bf16[320,320]{1,0:T(8,128)(2,1)}, u32[]{:S(2)}) copy-start(bf16[320,320]{1,0:T(8,128)(2,1)} %tmk_ref.1) | copy-start | bytes 614404
  1.4 3.0 %copy-start.6 = (bf16[320,320]{1,0:T(8,128)(2,1)S(1)}, bf16[320,320]{1,0:T(8,128)(2,1)}, u32[]{:S(2)}) copy-start(bf16[320,320]{1,0:T(8,128)(2,1)} %tmv_ref.1) | copy-start | bytes 614404
  1.4 3.0 %copy-start.7 = (bf16[320,320]{1,0:T(8,128)(2,1)S(1)}, bf16[320,320]{1,0:T(8,128)(2,1)}, u32[]{:S(2)}) copy-start(bf16[320,320]{1,0:T(8,128)(2,1)} %tmo_ref.1) | copy-start | bytes 614404
  2.6 1.7 %copy-start = (bf16[320,320]{1,0:T(8,128)(2,1)S(1)}, bf16[320,320]{1,0:T(8,128)(2,1)}, u32[]{:S(2)}) copy-start(bf16[320,320]{1,0:T(8,128)(2,1)} %spq_ref.1) | copy-start | bytes 614404
  2.7 1.7 %copy-start.1 = (bf16[320,320]{1,0:T(8,128)(2,1)S(1)}, bf16[320,320]{1,0:T(8,128)(2,1)}, u32[]{:S(2)}) copy-start(bf16[320,320]{1,0:T(8,128)(2,1)} %spk_ref.1) | copy-start | bytes 614404
  2.7 1.7 %copy-start.2 = (bf16[320,320]{1,0:T(8,128)(2,1)S(1)}, bf16[320,320]{1,0:T(8,128)(2,1)}, u32[]{:S(2)}) copy-start(bf16[320,320]{1,0:T(8,128)(2,1)} %spv_ref.1) | copy-start | bytes 614404
  2.7 1.7 %copy-start.3 = (bf16[320,320]{1,0:T(8,128)(2,1)S(1)}, bf16[320,320]{1,0:T(8,128)(2,1)}, u32[]{:S(2)}) copy-start(bf16[320,320]{1,0:T(8,128)(2,1)} %spo_ref.1) | copy-start | bytes 614404
  2.7 1.7 %copy-start.4 = (bf16[320,320]{1,0:T(8,128)(2,1)S(1)}, bf16[320,320]{1,0:T(8,128)(2,1)}, u32[]{:S(2)}) copy-start(bf16[320,320]{1,0:T(8,128)(2,1)} %tmq_ref.1) | copy-start | bytes 614404
  2.7 1.7 %copy-start.8 = (bf16[32,320]{1,0:T(8,128)(2,1)S(1)}, bf16[32,320]{1,0:T(8,128)(2,1)}, u32[]{:S(2)}) copy-start(bf16[32,320]{1,0:T(8,128)(2,1)} %ref_ref.1) | copy-start | bytes 61444
  4.3 0.7 %copy-start.9 = (s32[2]{0:T(128)S(1)}, s32[2]{0:T(128)}, u32[]{:S(2)}) copy-start(s32[2]{0:T(128)} %frame_ref.1) | copy-start | bytes 28

commit v2 on v1

--- a/solution.py
+++ b/solution.py
@@ -120,6 +120,19 @@
     )
 
 
+def layer_norm_down(values, gain):
+    mean = jnp.mean(values, axis=0, keepdims=True)
+    centered = values - mean
+    var = jnp.mean(centered * centered, axis=0, keepdims=True)
+    return centered * lax.rsqrt(var + 1e-05) * gain
+
+
+def project_down(weight, rows, contract):
+    return lax.dot_general(
+        weight, rows, (((0,), (contract,)), ((), ())), preferred_element_type=jnp.float32
+    )
+
+
 def head_span(head, head_dim, width):
     low = head * head_dim
     high = low + head_dim
@@ -190,10 +203,9 @@
     q_buf,
     k_buf,
     v_buf,
-    rk_buf,
-    rv_buf,
     mid_buf,
     pe_buf,
+    gain2_buf,
     fwd_out,
     fwd_in,
     bwd_out,
@@ -206,9 +218,11 @@
     bwd_recv,
 ):
     me = lax.axis_index("frame")
-    frames_here, _, halves, rows, width = hidden_ref.shape
+    frames_here, width, positions = hidden_ref.shape
+    halves, rows = fwd_out.shape[0], fwd_out.shape[3]
     count = blocks * rows
     frames = frames_here * blocks
+    head_dim = width // HEADS
     bf16 = jnp.bfloat16
 
     def peer(shift):
@@ -220,7 +234,7 @@
             barrier, inc=1, device_id={"frame": peer(shift)}, device_id_type=pl.DeviceIdType.MESH
         )
 
-    gain1 = gain1_ref[...]
+    gain1 = gain1_ref[...].reshape(1, width)
     ref_buf[me] = layer_norm(ref_ref[...].astype(jnp.float32), gain1).astype(bf16)
     pl.semaphore_wait(barrier, blocks - 1)
 
@@ -257,52 +271,76 @@
     for shift in range(1, blocks):
         ref_copy(shift).start()
 
-    step = step_ref[0]
-    rows8 = temb_ref[step // 8].astype(jnp.float32)
-    row_id = lax.broadcasted_iota(jnp.int32, rows8.shape, 0)
-    temb = jnp.sum(jnp.where(row_id == step % 8, rows8, 0.0), axis=0, keepdims=True)
+    def column(row):
+        return jnp.broadcast_to(row, (count, width)).T
+
+    steps = temb_ref.shape[1]
+    chosen = lax.broadcasted_iota(jnp.int32, (steps, count), 0) == step_ref[0]
+    temb = jnp.dot(
+        temb_ref[...],
+        jnp.where(chosen, 1.0, 0.0).astype(bf16),
+        preferred_element_type=jnp.float32,
+    )
 
     chan = lax.broadcasted_iota(jnp.int32, (1, width), 1)
     freq = jnp.exp(-(chan // 2 * 2).astype(jnp.float32) / width * math.log(10000.0))
     phase = (chan % 2).astype(jnp.float32) * (math.pi / 2)
     for f in range(frames_here):
-        pe_buf[f] = jnp.sin(frame_ref[f].astype(jnp.float32) * freq + phase)
-
+        pe_buf[f] = column(jnp.sin(frame_ref[f].astype(jnp.float32) * freq + phase))
+
+    gain1 = column(gain1)
     for f in range(frames_here):
         normed = []
         for half in range(halves):
-            base = hidden_ref[f, :, half].reshape(count, width).astype(jnp.float32) + temb
+            base = hidden_ref[f, :, half * count : (half + 1) * count].astype(jnp.float32) + temb
             mid_buf[half, f] = base
-            normed.append(layer_norm(base, gain1).astype(bf16))
-        normed = jnp.concatenate(normed, axis=0)
-        query = project(normed, spq_ref[...])
+            normed.append(layer_norm_down(base, gain1).astype(bf16))
+        normed = jnp.concatenate(normed, axis=1)
+        query = project_down(spq_ref[...], normed, 0)
         for half in range(halves):
-            q_buf[half, f] = query[half * count : (half + 1) * count]
-        k_buf[f] = project(normed, spk_ref[...])
-        v_buf[f] = project(normed, spv_ref[...])
+            for head in range(HEADS):
+                low, high, first, last = head_span(head, head_dim, width)
+                piece = query[first:last, half * count : (half + 1) * count]
+                row = lax.broadcasted_iota(jnp.int32, piece.shape, 0) + first
+                piece = jnp.where((row >= low) & (row < high), piece, 0.0)
+                q_buf[half, f, head, : last - first] = piece.astype(bf16)
+        k_buf[f, :positions] = project(normed.T, spk_ref[...])
+        value = project_down(spv_ref[...], normed, 0)
+        v_buf[f, :, :, :positions] = value.reshape(HEADS, head_dim, positions).astype(bf16)
 
     for shift in range(1, blocks):
         ref_copy(shift).wait_recv()
     ref_all = ref_buf[...].reshape(-1, width)
-    rk_buf[...] = project(ref_all, spk_ref[...])
-    rv_buf[...] = project(ref_all, spv_ref[...])
-
-    gain2 = gain2_ref[...]
+    ref_key = project(ref_all, spk_ref[...])
+    ref_value = project_down(spv_ref[...], ref_all, 1)
+    ref_value = ref_value.reshape(HEADS, head_dim, positions).astype(bf16)
+    for f in range(frames_here):
+        k_buf[f, positions:] = ref_key
+        v_buf[f, :, :, positions:] = ref_value
+
+    gain2_buf[...] = column(gain2_ref[...].reshape(1, width))
+    factor = math.log2(math.e) / math.sqrt(head_dim)
 
     def spatial(half, carry):
         for f in range(frames_here):
-            attn = attend_heads(
-                q_buf[half, f],
-                [lambda a, b: k_buf[f, :, a:b], lambda a, b: rk_buf[:, a:b]],
-                [lambda a, b: v_buf[f, :, a:b], lambda a, b: rv_buf[:, a:b]],
-                width,
-            ).astype(bf16)
-            mid = mid_buf[half, f] + jnp.dot(
-                attn, spo_ref[...], preferred_element_type=jnp.float32
-            )
+            done = []
+            for head in range(HEADS):
+                low, high, first, last = head_span(head, head_dim, width)
+                scores = jnp.dot(
+                    k_buf[f, :, first:last],
+                    q_buf[half, f, head, : last - first],
+                    preferred_element_type=jnp.float32,
+                )
+                top = jnp.max(scores, axis=0, keepdims=True)
+                exps = jnp.exp2((scores - top) * factor)
+                inverse = 1.0 / jnp.sum(exps, axis=0, keepdims=True)
+                probs = (exps * inverse).astype(bf16)
+                done.append(jnp.dot(v_buf[f, head], probs, preferred_element_type=jnp.float32))
+            attn = jnp.concatenate(done, axis=0).astype(bf16)
+            mid = mid_buf[half, f] + project_down(spo_ref[...], attn, 0)
             mid_buf[half, f] = mid
-            normed = (layer_norm(mid, gain2) + pe_buf[f]).astype(bf16)
-            fwd_out[half, :, f] = normed.reshape(blocks, rows, width)
+            normed = layer_norm_down(mid, gain2_buf[...]) + pe_buf[f]
+            fwd_out[half, :, f] = normed.T.astype(bf16).reshape(blocks, rows, width)
         for shift in range(1, blocks):
             fwd_copy(half, shift).start()
         fwd_in[half, me] = fwd_out[half, me]
@@ -346,18 +384,13 @@
 
     lax.fori_loop(0, halves, temporal, 0)
 
-    def finish(half, carry):
+    for half in range(halves):
         for shift in range(1, blocks):
             bwd_copy(half, shift).wait_recv()
         for f in range(frames_here):
             attn = bwd_in[half, :, f].reshape(count, width)
-            mixed = mid_buf[half, f] + jnp.dot(
-                attn, tmo_ref[...], preferred_element_type=jnp.float32
-            )
-            out_ref[f, :, half] = mixed.astype(bf16).reshape(blocks, rows, width)
-        return carry
-
-    lax.fori_loop(0, halves, finish, 0)
+            mixed = mid_buf[half, f] + project_down(tmo_ref[...], attn, 1)
+            out_ref[f, :, half * count : (half + 1) * count] = mixed.astype(bf16)
 
     for shift in range(1, blocks):
         ref_copy(shift).wait_send()
@@ -390,18 +423,17 @@
     moved = (halves, blocks, frames_here, rows, width)
     out = pl.pallas_call(
         functools.partial(fused_kernel, blocks),
-        out_shape=jax.ShapeDtypeStruct((frames_here, blocks, halves, rows, width), bf16),
+        out_shape=jax.ShapeDtypeStruct((frames_here, width, positions), bf16),
         in_specs=[smem, smem] + [vmem] * 13,
         out_specs=vmem,
         scratch_shapes=[
             pltpu.VMEM((blocks, ref_rows, width), bf16),
-            pltpu.VMEM((halves, frames_here, count, width), bf16),
-            pltpu.VMEM((frames_here, positions, width), bf16),
-            pltpu.VMEM((frames_here, positions, width), bf16),
-            pltpu.VMEM((blocks * ref_rows, width), bf16),
-            pltpu.VMEM((blocks * ref_rows, width), bf16),
-            pltpu.VMEM((halves, frames_here, count, width), jnp.float32),
-            pltpu.VMEM((frames_here, 1, width), jnp.float32),
+            pltpu.VMEM((halves, frames_here, HEADS, 256, count), bf16),
+            pltpu.VMEM((frames_here, 2 * positions, width), bf16),
+            pltpu.VMEM((frames_here, HEADS, width // HEADS, 2 * positions), bf16),
+            pltpu.VMEM((halves, frames_here, width, count), jnp.float32),
+            pltpu.VMEM((frames_here, width, count), jnp.float32),
+            pltpu.VMEM((width, count), jnp.float32),
             pltpu.VMEM(moved, bf16),
             pltpu.VMEM(moved, bf16),
             pltpu.VMEM(moved, bf16),
@@ -419,24 +451,23 @@
     )(
         step_index,
         frame_index,
-        hidden.reshape(frames_here, blocks, halves, rows, width),
+        hidden.transpose(0, 2, 1),
         ref_feats,
-        temb_table.reshape(-1, 8, width),
-        norm_gain_1.reshape(1, width),
-        norm_gain_2.reshape(1, width),
+        temb_table.T,
+        norm_gain_1,
+        norm_gain_2,
         *weights,
     )
-    return out.reshape(frames_here, positions, width)
+    return out.transpose(0, 2, 1)
 
 
 def on_device(hidden, ref_feats, frame_index, step_index, temb_table, *rest):
     blocks = lax.axis_size("frame")
     frames_here, positions, width = hidden.shape
     fits = (
-        positions % (32 * blocks) == 0
+        positions == 256 and positions % (32 * blocks) == 0
         and blocks * ref_feats.shape[0] == positions
         and ref_feats.shape[0] % 16 == 0
-        and temb_table.shape[0] % 8 == 0
         and frames_here * blocks * 8 <= 128
     )
     body = on_device_fused if fits else on_device_plain

time: 45.5 us -> 52.5 us (1.15)
  local copies, waits for them, and re-layouts: 5.05 us -> 11.7 us
    unnamed x24 -> x29, local copies, waits for them, and re-layouts: 3.45 us -> 11.7 us
    reshape x3 -> x0, local copies, waits for them, and re-layouts: 1.6 us -> none  [the longest x1 0.91 us: on_device_fused(): return out.reshape(frames_here, positions, width)]
where the time goes in v2:
time: 52.5 us; the launch traced here: 52 us
  Pallas kernels  39.5 us (75%)
  local copies, waits for them, and re-layouts  11.7 us (22%)
  between operations  0.71 us (1%)
    pallas_call x1, Pallas kernels, on_device_fused(): pl.pallas_call(functools.partial(fused_kernel, blocks), out_shape=jax.Sha...  39.5 us
    unnamed x29, local copies, waits for them, and re-layouts  11.7 us

profile of v2, /device:TPU:0, one launch (start us, length us, event | category | flops | bytes accessed | tf_op | source)
XLA Modules:
  0.0 52.0 jit_solution(12177669657590142706)
XLA Ops:
  0.0 0.0 copy-start.12
  0.7 0.0 copy-start.11
  0.7 0.0 copy-start.13
  0.7 0.0 copy-done.12
  0.7 0.7 %copy-done.11 = f32[320]{0:T(512)S(1)} copy-done((f32[320]{0:T(512)S(1)}, f32[320]{0:T(512)}, u32[]{:S(2)}) %copy-start.11) | copy-done | bytes 1304
  1.4 0.0 copy-done.13
  1.4 0.0 copy-start
  1.4 1.1 %copy-done = bf16[1000,320]{0,1:T(8,128)(2,1)S(1)} copy-done((bf16[1000,320]{0,1:T(8,128)(2,1)S(1)}, bf16[1000,320]{0,1:T(8,128)(2,1)}, u32[]{:S(2)}) %copy-start) | copy-done | bytes 640024
  2.4 0.0 copy-start.1
  2.4 1.0 %copy-done.1 = bf16[2,256,320]{1,2,0:T(8,128)(2,1)S(1)} copy-done((bf16[2,256,320]{1,2,0:T(8,128)(2,1)S(1)}, bf16[2,256,320]{1,2,0:T(8,128)(2,1)}, u32[]{:S(2)}) %copy-start.1) | copy-done | bytes 327704
  3.4 0.0 copy-start.2
  3.4 0.9 %copy-done.2 = bf16[320,320]{1,0:T(8,128)(2,1)S(1)} copy-done((bf16[320,320]{1,0:T(8,128)(2,1)S(1)}, bf16[320,320]{1,0:T(8,128)(2,1)}, u32[]{:S(2)}) %copy-start.2) | copy-done | bytes 204824
  4.4 0.0 copy-start.3
  4.4 0.9 %copy-done.3 = bf16[320,320]{1,0:T(8,128)(2,1)S(1)} copy-done((bf16[320,320]{1,0:T(8,128)(2,1)S(1)}, bf16[320,320]{1,0:T(8,128)(2,1)}, u32[]{:S(2)}) %copy-start.3) | copy-done | bytes 204824
  5.3 0.0 copy-start.4
  5.3 0.9 %copy-done.4 = bf16[320,320]{1,0:T(8,128)(2,1)S(1)} copy-done((bf16[320,320]{1,0:T(8,128)(2,1)S(1)}, bf16[320,320]{1,0:T(8,128)(2,1)}, u32[]{:S(2)}) %copy-start.4) | copy-done | bytes 204824
  6.2 0.0 copy-start.5
  6.3 0.9 %copy-done.5 = bf16[320,320]{1,0:T(8,128)(2,1)S(1)} copy-done((bf16[320,320]{1,0:T(8,128)(2,1)S(1)}, bf16[320,320]{1,0:T(8,128)(2,1)}, u32[]{:S(2)}) %copy-start.5) | copy-done | bytes 204824
  7.2 0.0 copy-start.6
  7.2 0.9 %copy-done.6 = bf16[320,320]{1,0:T(8,128)(2,1)S(1)} copy-done((bf16[320,320]{1,0:T(8,128)(2,1)S(1)}, bf16[320,320]{1,0:T(8,128)(2,1)}, u32[]{:S(2)}) %copy-start.6) | copy-done | bytes 204824
  8.1 0.0 copy-start.7
  8.1 0.9 %copy-done.7 = bf16[320,320]{1,0:T(8,128)(2,1)S(1)} copy-done((bf16[320,320]{1,0:T(8,128)(2,1)S(1)}, bf16[320,320]{1,0:T(8,128)(2,1)}, u32[]{:S(2)}) %copy-start.7) | copy-done | bytes 204824
  9.1 0.0 copy-start.8
  9.1 0.9 %copy-done.8 = bf16[320,320]{1,0:T(8,128)(2,1)S(1)} copy-done((bf16[320,320]{1,0:T(8,128)(2,1)S(1)}, bf16[320,320]{1,0:T(8,128)(2,1)}, u32[]{:S(2)}) %copy-start.8) | copy-done | bytes 204824
  10.0 0.0 copy-start.9
  10.0 0.9 %copy-done.9 = bf16[320,320]{1,0:T(8,128)(2,1)S(1)} copy-done((bf16[320,320]{1,0:T(8,128)(2,1)S(1)}, bf16[320,320]{1,0:T(8,128)(2,1)}, u32[]{:S(2)}) %copy-start.9) | copy-done | bytes 204824
  11.0 0.0 copy-start.10
  11.0 0.7 %copy-done.10 = bf16[32,320]{1,0:T(8,128)(2,1)S(1)} copy-done((bf16[32,320]{1,0:T(8,128)(2,1)S(1)}, bf16[32,320]{1,0:T(8,128)(2,1)}, u32[]{:S(2)}) %copy-start.10) | copy-done | bytes 20504
  11.7 39.5 %shard_map.145 = bf16[2,320,256]{2,1,0:T(8,128)(2,1)S(1)} custom-call(s32[1]{0:T(128)S(6)} %copy.17.step_ref, s32[2]{0:T(128)S(1)} %copy-done.13, bf16[2,320,256]{2,1,0:T(8,128)(2,1)S(1)} %bitcast.5, bf16[32,320]{1,0:T(8,128)(2,1)S(1)} %copy-done.10, bf16[320,1000]{1,0:T(8,128)(2,1)S(1)} %bitcast.4, f32[320]{0:T(512)S(1)} %copy-done.11, f32[320]{0:T(512)S(1)} %copy-done.12, ...), custom_call_target="tpu_custom_call" | custom-call | tf_op jit(solution)/shard_map/pallas_call | solution.py:424
  51.2 0.7 %copy.18 = bf16[2,256,320]{1,2,0:T(8,128)(2,1)} copy(bf16[2,256,320]{1,2,0:T(8,128)(2,1)S(1)} %bitcast.3) | data formatting | bytes 655360
Async XLA Ops:
  0.0 0.7 %copy-start.12 = (f32[320]{0:T(512)S(1)}, f32[320]{0:T(512)}, u32[]{:S(2)}) copy-start(f32[320]{0:T(512)} %gain2_ref.1) | copy-start | bytes 3844
  0.7 0.7 %copy-start.11 = (f32[320]{0:T(512)S(1)}, f32[320]{0:T(512)}, u32[]{:S(2)}) copy-start(f32[320]{0:T(512)} %gain1_ref.1) | copy-start | bytes 3844
  0.7 0.7 %copy-start.13 = (s32[2]{0:T(128)S(1)}, s32[2]{0:T(128)}, u32[]{:S(2)}) copy-start(s32[2]{0:T(128)} %frame_ref.1) | copy-start | bytes 28
  1.4 1.1 %copy-start = (bf16[1000,320]{0,1:T(8,128)(2,1)S(1)}, bf16[1000,320]{0,1:T(8,128)(2,1)}, u32[]{:S(2)}) copy-start(bf16[1000,320]{0,1:T(8,128)(2,1)} %param.19) | copy-start | bytes 1920004
  2.4 1.0 %copy-start.1 = (bf16[2,256,320]{1,2,0:T(8,128)(2,1)S(1)}, bf16[2,256,320]{1,2,0:T(8,128)(2,1)}, u32[]{:S(2)}) copy-start(bf16[2,256,320]{1,2,0:T(8,128)(2,1)} %param.15) | copy-start | bytes 983044
  3.4 0.9 %copy-start.2 = (bf16[320,320]{1,0:T(8,128)(2,1)S(1)}, bf16[320,320]{1,0:T(8,128)(2,1)}, u32[]{:S(2)}) copy-start(bf16[320,320]{1,0:T(8,128)(2,1)} %spq_ref.1) | copy-start | bytes 614404
  4.4 0.9 %copy-start.3 = (bf16[320,320]{1,0:T(8,128)(2,1)S(1)}, bf16[320,320]{1,0:T(8,128)(2,1)}, u32[]{:S(2)}) copy-start(bf16[320,320]{1,0:T(8,128)(2,1)} %spk_ref.1) | copy-start | bytes 614404
  5.3 0.9 %copy-start.4 = (bf16[320,320]{1,0:T(8,128)(2,1)S(1)}, bf16[320,320]{1,0:T(8,128)(2,1)}, u32[]{:S(2)}) copy-start(bf16[320,320]{1,0:T(8,128)(2,1)} %spv_ref.1) | copy-start | bytes 614404
  6.2 0.9 %copy-start.5 = (bf16[320,320]{1,0:T(8,128)(2,1)S(1)}, bf16[320,320]{1,0:T(8,128)(2,1)}, u32[]{:S(2)}) copy-start(bf16[320,320]{1,0:T(8,128)(2,1)} %spo_ref.1) | copy-start | bytes 614404
  7.2 0.9 %copy-start.6 = (bf16[320,320]{1,0:T(8,128)(2,1)S(1)}, bf16[320,320]{1,0:T(8,128)(2,1)}, u32[]{:S(2)}) copy-start(bf16[320,320]{1,0:T(8,128)(2,1)} %tmq_ref.1) | copy-start | bytes 614404
  8.1 0.9 %copy-start.7 = (bf16[320,320]{1,0:T(8,128)(2,1)S(1)}, bf16[320,320]{1,0:T(8,128)(2,1)}, u32[]{:S(2)}) copy-start(bf16[320,320]{1,0:T(8,128)(2,1)} %tmk_ref.1) | copy-start | bytes 614404
  9.1 0.9 %copy-start.8 = (bf16[320,320]{1,0:T(8,128)(2,1)S(1)}, bf16[320,320]{1,0:T(8,128)(2,1)}, u32[]{:S(2)}) copy-start(bf16[320,320]{1,0:T(8,128)(2,1)} %tmv_ref.1) | copy-start | bytes 614404
  10.0 0.9 %copy-start.9 = (bf16[320,320]{1,0:T(8,128)(2,1)S(1)}, bf16[320,320]{1,0:T(8,128)(2,1)}, u32[]{:S(2)}) copy-start(bf16[320,320]{1,0:T(8,128)(2,1)} %tmo_ref.1) | copy-start | bytes 614404
  11.0 0.7 %copy-start.10 = (bf16[32,320]{1,0:T(8,128)(2,1)S(1)}, bf16[32,320]{1,0:T(8,128)(2,1)}, u32[]{:S(2)}) copy-start(bf16[32,320]{1,0:T(8,128)(2,1)} %ref_ref.1) | copy-start | bytes 61444

commit v3 on v2

--- a/solution.py
+++ b/solution.py
@@ -183,6 +183,22 @@
 
 def fused_kernel(
     blocks,
+    step_hbm,
+    frame_hbm,
+    hidden_hbm,
+    ref_hbm,
+    temb_hbm,
+    gain1_hbm,
+    gain2_hbm,
+    spq_hbm,
+    spk_hbm,
+    spv_hbm,
+    spo_hbm,
+    tmq_hbm,
+    tmk_hbm,
+    tmv_hbm,
+    tmo_hbm,
+    out_ref,
     step_ref,
     frame_ref,
     hidden_ref,
@@ -198,7 +214,7 @@
     tmk_ref,
     tmv_ref,
     tmo_ref,
-    out_ref,
+    load_sem,
     ref_buf,
     q_buf,
     k_buf,
@@ -228,12 +244,39 @@
     def peer(shift):
         return lax.rem(me + shift, blocks)
 
+    loads = [
+        pltpu.make_async_copy(source, target, load_sem.at[place])
+        for place, (source, target) in enumerate(
+            (
+                (ref_hbm, ref_ref),
+                (gain1_hbm, gain1_ref),
+                (step_hbm, step_ref),
+                (frame_hbm, frame_ref),
+                (temb_hbm, temb_ref),
+                (hidden_hbm, hidden_ref),
+                (spq_hbm, spq_ref),
+                (spk_hbm, spk_ref),
+                (spv_hbm, spv_ref),
+                (gain2_hbm, gain2_ref),
+                (spo_hbm, spo_ref),
+                (tmq_hbm, tmq_ref),
+                (tmk_hbm, tmk_ref),
+                (tmv_hbm, tmv_ref),
+                (tmo_hbm, tmo_ref),
+            )
+        )
+    ]
+    for load in loads:
+        load.start()
+
     barrier = pltpu.get_barrier_semaphore()
     for shift in range(1, blocks):
         pl.semaphore_signal(
             barrier, inc=1, device_id={"frame": peer(shift)}, device_id_type=pl.DeviceIdType.MESH
         )
 
+    for load in loads[:2]:
+        load.wait()
     gain1 = gain1_ref[...].reshape(1, width)
     ref_buf[me] = layer_norm(ref_ref[...].astype(jnp.float32), gain1).astype(bf16)
     pl.semaphore_wait(barrier, blocks - 1)
@@ -274,6 +317,8 @@
     def column(row):
         return jnp.broadcast_to(row, (count, width)).T
 
+    for load in loads[2:]:
+        load.wait()
     steps = temb_ref.shape[1]
     chosen = lax.broadcasted_iota(jnp.int32, (steps, count), 0) == step_ref[0]
     temb = jnp.dot(
@@ -322,15 +367,22 @@
     factor = math.log2(math.e) / math.sqrt(head_dim)
 
     def spatial(half, carry):
+        def score(f, head):
+            low, high, first, last = head_span(head, head_dim, width)
+            return jnp.dot(
+                k_buf[f, :, first:last],
+                q_buf[half, f, head, : last - first],
+                preferred_element_type=jnp.float32,
+            )
+
+        units = [(f, head) for f in range(frames_here) for head in range(HEADS)]
+        ahead = score(*units[0])
         for f in range(frames_here):
             done = []
             for head in range(HEADS):
-                low, high, first, last = head_span(head, head_dim, width)
-                scores = jnp.dot(
-                    k_buf[f, :, first:last],
-                    q_buf[half, f, head, : last - first],
-                    preferred_element_type=jnp.float32,
-                )
+                scores = ahead
+                if f * HEADS + head + 1 < len(units):
+                    ahead = score(*units[f * HEADS + head + 1])
                 top = jnp.max(scores, axis=0, keepdims=True)
                 exps = jnp.exp2((scores - top) * factor)
                 inverse = 1.0 / jnp.sum(exps, axis=0, keepdims=True)
@@ -418,15 +470,26 @@
     ref_rows = ref_feats.shape[0]
     bf16 = jnp.bfloat16
     dma = pltpu.SemaphoreType.DMA
-    smem = pl.BlockSpec(memory_space=pltpu.SMEM)
-    vmem = pl.BlockSpec(memory_space=pltpu.VMEM)
+    args = (
+        step_index,
+        frame_index,
+        hidden.transpose(0, 2, 1),
+        ref_feats,
+        temb_table.T,
+        norm_gain_1,
+        norm_gain_2,
+        *weights,
+    )
     moved = (halves, blocks, frames_here, rows, width)
     out = pl.pallas_call(
         functools.partial(fused_kernel, blocks),
         out_shape=jax.ShapeDtypeStruct((frames_here, width, positions), bf16),
-        in_specs=[smem, smem] + [vmem] * 13,
-        out_specs=vmem,
-        scratch_shapes=[
+        in_specs=[pl.BlockSpec(memory_space=pltpu.HBM)] * len(args),
+        out_specs=pl.BlockSpec(memory_space=pltpu.VMEM),
+        scratch_shapes=[pltpu.SMEM(a.shape, a.dtype) for a in args[:2]]
+        + [pltpu.VMEM(a.shape, a.dtype) for a in args[2:]]
+        + [
+            dma((len(args),)),
             pltpu.VMEM((blocks, ref_rows, width), bf16),
             pltpu.VMEM((halves, frames_here, HEADS, 256, count), bf16),
             pltpu.VMEM((frames_here, 2 * positions, width), bf16),
@@ -446,18 +509,9 @@
             dma((halves, blocks - 1)),
         ],
         compiler_params=pltpu.CompilerParams(
-            collective_id=0, has_side_effects=True, vmem_limit_bytes=32 * 1024 * 1024
+            collective_id=0, has_side_effects=True, vmem_limit_bytes=60 * 1024 * 1024
         ),
-    )(
-        step_index,
-        frame_index,
-        hidden.transpose(0, 2, 1),
-        ref_feats,
-        temb_table.T,
-        norm_gain_1,
-        norm_gain_2,
-        *weights,
-    )
+    )(*args)
     return out.transpose(0, 2, 1)
 
 

time: 52.5 us -> 41.4 us (0.79)
  local copies, waits for them, and re-layouts: 11.7 us -> 1.72 us
  Pallas kernels: 39.5 us -> 38.8 us
    unnamed x29 -> x1, local copies, waits for them, and re-layouts: 11.7 us -> 1.72 us
    pallas_call x1, Pallas kernels: 39.5 us -> 38.8 us  [on_device_fused(): pl.pallas_call(functools.partial(fused_kernel, blocks), out_shape=jax.Sha...]
where the time goes in v3:
time: 41.4 us; the launch traced here: 41.2 us
  Pallas kernels  38.8 us (94%)
  local copies, waits for them, and re-layouts  1.72 us (4%)
  between operations  0.66 us (2%)
    pallas_call x1, Pallas kernels, on_device_fused(): pl.pallas_call(functools.partial(fused_kernel, blocks), out_shape=jax.Sha...  38.8 us
    unnamed x1, local copies, waits for them, and re-layouts  1.72 us

profile of v3, /device:TPU:0, one launch (start us, length us, event | category | flops | bytes accessed | tf_op | source)
XLA Modules:
  0.0 41.2 jit_solution(11451351804958989887)
XLA Ops:
  0.7 38.8 %shard_map.145 = bf16[2,320,256]{2,1,0:T(8,128)(2,1)} custom-call(s32[1]{0:T(128)S(6)} %copy.17.step_hbm, s32[2]{0:T(128)} %frame_hbm.1, bf16[2,320,256]{2,1,0:T(8,128)(2,1)} %bitcast.5, bf16[32,320]{1,0:T(8,128)(2,1)} %ref_hbm.1, bf16[320,1000]{1,0:T(8,128)(2,1)} %bitcast.4, f32[320]{0:T(512)} %gain1_hbm.1, f32[320]{0:T(512)} %gain2_hbm.1, ...), custom_call_target="tpu_custom_call" | custom-call | tf_op jit(solution)/shard_map/pallas_call | solution.py:484
  39.5 1.7 %copy.18 = bf16[2,256,320]{1,2,0:T(8,128)(2,1)} copy(bf16[2,256,320]{1,2,0:T(8,128)(2,1)} %bitcast.3) | data formatting | bytes 655360

commit v4 on v3

--- a/solution.py
+++ b/solution.py
@@ -235,7 +235,7 @@
 ):
     me = lax.axis_index("frame")
     frames_here, width, positions = hidden_ref.shape
-    halves, rows = fwd_out.shape[0], fwd_out.shape[3]
+    halves, rows = fwd_out.shape[0], fwd_out.shape[2]
     count = blocks * rows
     frames = frames_here * blocks
     head_dim = width // HEADS
@@ -291,15 +291,25 @@
             device_id_type=pl.DeviceIdType.MESH,
         )
 
-    def fwd_copy(half, shift):
+    whole = width // 128 * 128
+    lanes = (pl.ds(0, whole), pl.ds(whole, 2 * width - whole))
+
+    def fwd_copy(half, f, shift):
         return pltpu.make_async_remote_copy(
-            src_ref=fwd_out.at[half, peer(shift)],
-            dst_ref=fwd_in.at[half, me],
-            send_sem=fwd_send.at[half, shift - 1],
-            recv_sem=fwd_recv.at[half, shift - 1],
+            src_ref=fwd_out.at[half, peer(shift), :, lanes[f]],
+            dst_ref=fwd_in.at[half, me, :, lanes[f]],
+            send_sem=fwd_send.at[half, f, shift - 1],
+            recv_sem=fwd_recv.at[half, f, shift - 1],
             device_id={"frame": peer(shift)},
             device_id_type=pl.DeviceIdType.MESH,
         )
+
+    def pack(first, second):
+        return jnp.concatenate([first, second[..., whole:], second[..., :whole]], axis=-1)
+
+    def unpack(both):
+        second = [both[..., 2 * width - whole :], both[..., width : 2 * width - whole]]
+        return both[..., :width], jnp.concatenate(second, axis=-1)
 
     def bwd_copy(half, shift):
         return pltpu.make_async_remote_copy(
@@ -392,9 +402,16 @@
             mid = mid_buf[half, f] + project_down(spo_ref[...], attn, 0)
             mid_buf[half, f] = mid
             normed = layer_norm_down(mid, gain2_buf[...]) + pe_buf[f]
-            fwd_out[half, :, f] = normed.T.astype(bf16).reshape(blocks, rows, width)
-        for shift in range(1, blocks):
-            fwd_copy(half, shift).start()
+            normed = normed.T.astype(bf16).reshape(blocks, rows, width)
+            if f == 0:
+                first_tail = normed[:, :, whole:]
+                fwd_out[half, :, :, :whole] = normed[:, :, :whole]
+            else:
+                fwd_out[half, :, :, whole:] = jnp.concatenate(
+                    [first_tail, normed[:, :, whole:], normed[:, :, :whole]], axis=-1
+                )
+            for shift in range(1, blocks):
+                fwd_copy(half, f, shift).start()
         fwd_in[half, me] = fwd_out[half, me]
         return carry
 
@@ -408,8 +425,9 @@
 
     def temporal(half, carry):
         for shift in range(1, blocks):
-            fwd_copy(half, shift).wait_recv()
-        normed = fwd_in[half].reshape(frames * rows, width)
+            for f in range(frames_here):
+                fwd_copy(half, f, shift).wait_recv()
+        normed = jnp.concatenate(unpack(fwd_in[half]), axis=0).reshape(frames * rows, width)
 
         def grouped(weight_ref):
             full = jnp.dot(normed, weight_ref[...], preferred_element_type=jnp.float32)
@@ -427,8 +445,8 @@
                 same,
             )
             done.append(attn.reshape(frames, 1, group, width))
-        attn = jnp.concatenate(done, axis=1).reshape(blocks, frames_here, rows, width)
-        bwd_out[half] = attn.astype(bf16)
+        attn = jnp.concatenate(done, axis=1).reshape(frames, rows, width).astype(bf16)
+        bwd_out[half] = pack(attn[:blocks], attn[blocks:])
         for shift in range(1, blocks):
             bwd_copy(half, shift).start()
         bwd_in[half, me] = bwd_out[half, me]
@@ -439,15 +457,16 @@
     for half in range(halves):
         for shift in range(1, blocks):
             bwd_copy(half, shift).wait_recv()
-        for f in range(frames_here):
-            attn = bwd_in[half, :, f].reshape(count, width)
+        for f, attn in enumerate(unpack(bwd_in[half])):
+            attn = attn.reshape(count, width)
             mixed = mid_buf[half, f] + project_down(tmo_ref[...], attn, 1)
             out_ref[f, :, half * count : (half + 1) * count] = mixed.astype(bf16)
 
     for shift in range(1, blocks):
         ref_copy(shift).wait_send()
         for half in range(halves):
-            fwd_copy(half, shift).wait_send()
+            for f in range(frames_here):
+                fwd_copy(half, f, shift).wait_send()
             bwd_copy(half, shift).wait_send()
 
 
@@ -480,7 +499,7 @@
         norm_gain_2,
         *weights,
     )
-    moved = (halves, blocks, frames_here, rows, width)
+    moved = (halves, blocks, rows, frames_here * width)
     out = pl.pallas_call(
         functools.partial(fused_kernel, blocks),
         out_shape=jax.ShapeDtypeStruct((frames_here, width, positions), bf16),
@@ -503,8 +522,8 @@
             pltpu.VMEM(moved, bf16),
             dma((blocks - 1,)),
             dma((blocks - 1,)),
-            dma((halves, blocks - 1)),
-            dma((halves, blocks - 1)),
+            dma((halves, frames_here, blocks - 1)),
+            dma((halves, frames_here, blocks - 1)),
             dma((halves, blocks - 1)),
             dma((halves, blocks - 1)),
         ],
@@ -519,7 +538,10 @@
     blocks = lax.axis_size("frame")
     frames_here, positions, width = hidden.shape
     fits = (
-        positions == 256 and positions % (32 * blocks) == 0
+        positions == 256
+        and positions % (32 * blocks) == 0
+        and frames_here == 2
+        and 2 * width % 128 == 0
         and blocks * ref_feats.shape[0] == positions
         and ref_feats.shape[0] % 16 == 0
         and frames_here * blocks * 8 <= 128

time: 41.4 us -> 38 us (0.918)
  Pallas kernels: 38.8 us -> 35.4 us
    pallas_call x1, Pallas kernels: 38.8 us -> 35.4 us  [on_device_fused(): pl.pallas_call(functools.partial(fused_kernel, blocks), out_shape=jax.Sha...]
where the time goes in v4:
time: 38 us; the launch traced here: 37.8 us
  Pallas kernels  35.4 us (93%)
  local copies, waits for them, and re-layouts  1.72 us (5%)
  between operations  0.66 us (2%)
    pallas_call x1, Pallas kernels, on_device_fused(): pl.pallas_call(functools.partial(fused_kernel, blocks), out_shape=jax.Sha...  35.4 us
    unnamed x1, local copies, waits for them, and re-layouts  1.72 us

profile of v4, /device:TPU:0, one launch (start us, length us, event | category | flops | bytes accessed | tf_op | source)
XLA Modules:
  0.0 37.8 jit_solution(14022656722227396941)
XLA Ops:
  0.7 35.4 %shard_map.145 = bf16[2,320,256]{2,1,0:T(8,128)(2,1)} custom-call(s32[1]{0:T(128)S(6)} %copy.17.step_hbm, s32[2]{0:T(128)} %frame_hbm.1, bf16[2,320,256]{2,1,0:T(8,128)(2,1)} %bitcast.5, bf16[32,320]{1,0:T(8,128)(2,1)} %ref_hbm.1, bf16[320,1000]{1,0:T(8,128)(2,1)} %bitcast.4, f32[320]{0:T(512)} %gain1_hbm.1, f32[320]{0:T(512)} %gain2_hbm.1, ...), custom_call_target="tpu_custom_call" | custom-call | tf_op jit(solution)/shard_map/pallas_call | solution.py:503
  36.1 1.7 %copy.18 = bf16[2,256,320]{1,2,0:T(8,128)(2,1)} copy(bf16[2,256,320]{1,2,0:T(8,128)(2,1)} %bitcast.3) | data formatting | bytes 655360

commit v5 on v4

--- a/solution.py
+++ b/solution.py
@@ -198,7 +198,9 @@
     tmk_hbm,
     tmv_hbm,
     tmo_hbm,
+    out_hbm,
     out_ref,
+    store_sem,
     step_ref,
     frame_ref,
     hidden_ref,
@@ -343,6 +345,32 @@
     for f in range(frames_here):
         pe_buf[f] = column(jnp.sin(frame_ref[f].astype(jnp.float32) * freq + phase))
 
+    pair_shape = (HEADS // 2, 2 * head_dim, positions)
+
+    def pair_span(pair):
+        _, _, first, _ = head_span(2 * pair, head_dim, width)
+        _, _, _, last = head_span(2 * pair + 1, head_dim, width)
+        return first, last
+
+    def by_head(pair, piece):
+        row = lax.broadcasted_iota(jnp.int32, piece.shape, 0) + pair_span(pair)[0]
+        start = 2 * pair * head_dim
+        middle, end = start + head_dim, start + 2 * head_dim
+        one = jnp.where((row >= start) & (row < middle), piece, 0.0)
+        two = jnp.where((row >= middle) & (row < end), piece, 0.0)
+        return jnp.concatenate([one, two], axis=1).astype(bf16)
+
+    def weigh(scores):
+        top = jnp.max(scores, axis=0, keepdims=True)
+        exps = jnp.exp2((scores - top) * factor)
+        inverse = 1.0 / jnp.sum(exps, axis=0, keepdims=True)
+        return (exps * inverse).astype(bf16)
+
+    def own_rows(values, probs):
+        both = jnp.dot(values, probs, preferred_element_type=jnp.float32)
+        return [both[:head_dim, :count], both[head_dim:, count:]]
+
+    factor = math.log2(math.e) / math.sqrt(head_dim)
     gain1 = column(gain1)
     for f in range(frames_here):
         normed = []
@@ -353,51 +381,45 @@
         normed = jnp.concatenate(normed, axis=1)
         query = project_down(spq_ref[...], normed, 0)
         for half in range(halves):
-            for head in range(HEADS):
-                low, high, first, last = head_span(head, head_dim, width)
+            for pair in range(HEADS // 2):
+                first, last = pair_span(pair)
                 piece = query[first:last, half * count : (half + 1) * count]
-                row = lax.broadcasted_iota(jnp.int32, piece.shape, 0) + first
-                piece = jnp.where((row >= low) & (row < high), piece, 0.0)
-                q_buf[half, f, head, : last - first] = piece.astype(bf16)
+                q_buf[half, f, pair, : last - first] = by_head(pair, piece)
         k_buf[f, :positions] = project(normed.T, spk_ref[...])
         value = project_down(spv_ref[...], normed, 0)
-        v_buf[f, :, :, :positions] = value.reshape(HEADS, head_dim, positions).astype(bf16)
+        v_buf[f, :, :, :positions] = value.reshape(pair_shape).astype(bf16)
 
     for shift in range(1, blocks):
         ref_copy(shift).wait_recv()
     ref_all = ref_buf[...].reshape(-1, width)
     ref_key = project(ref_all, spk_ref[...])
     ref_value = project_down(spv_ref[...], ref_all, 1)
-    ref_value = ref_value.reshape(HEADS, head_dim, positions).astype(bf16)
+    ref_value = ref_value.reshape(pair_shape).astype(bf16)
     for f in range(frames_here):
         k_buf[f, positions:] = ref_key
         v_buf[f, :, :, positions:] = ref_value
 
     gain2_buf[...] = column(gain2_ref[...].reshape(1, width))
-    factor = math.log2(math.e) / math.sqrt(head_dim)
 
     def spatial(half, carry):
-        def score(f, head):
-            low, high, first, last = head_span(head, head_dim, width)
+        def score(f, pair):
+            first, last = pair_span(pair)
             return jnp.dot(
                 k_buf[f, :, first:last],
-                q_buf[half, f, head, : last - first],
+                q_buf[half, f, pair, : last - first],
                 preferred_element_type=jnp.float32,
             )
 
-        units = [(f, head) for f in range(frames_here) for head in range(HEADS)]
+        units = [(f, pair) for f in range(frames_here) for pair in range(HEADS // 2)]
         ahead = score(*units[0])
         for f in range(frames_here):
             done = []
-            for head in range(HEADS):
+            for pair in range(HEADS // 2):
                 scores = ahead
-                if f * HEADS + head + 1 < len(units):
-                    ahead = score(*units[f * HEADS + head + 1])
-                top = jnp.max(scores, axis=0, keepdims=True)
-                exps = jnp.exp2((scores - top) * factor)
-                inverse = 1.0 / jnp.sum(exps, axis=0, keepdims=True)
-                probs = (exps * inverse).astype(bf16)
-                done.append(jnp.dot(v_buf[f, head], probs, preferred_element_type=jnp.float32))
+                place = units.index((f, pair)) + 1
+                if place < len(units):
+                    ahead = score(*units[place])
+                done += own_rows(v_buf[f, pair], weigh(scores))
             attn = jnp.concatenate(done, axis=0).astype(bf16)
             mid = mid_buf[half, f] + project_down(spo_ref[...], attn, 0)
             mid_buf[half, f] = mid
@@ -454,6 +476,7 @@
 
     lax.fori_loop(0, halves, temporal, 0)
 
+    stores = []
     for half in range(halves):
         for shift in range(1, blocks):
             bwd_copy(half, shift).wait_recv()
@@ -461,13 +484,36 @@
             attn = attn.reshape(count, width)
             mixed = mid_buf[half, f] + project_down(tmo_ref[...], attn, 1)
             out_ref[f, :, half * count : (half + 1) * count] = mixed.astype(bf16)
-
+            stores.append(
+                pltpu.make_async_copy(
+                    out_ref.at[f, :, pl.ds(half * count, count)],
+                    out_hbm.at[f, :, pl.ds(half * count, count)],
+                    store_sem.at[half, f],
+                )
+            )
+            stores[-1].start()
+
+    for store in stores:
+        store.wait()
     for shift in range(1, blocks):
         ref_copy(shift).wait_send()
         for half in range(halves):
             for f in range(frames_here):
                 fwd_copy(half, f, shift).wait_send()
             bwd_copy(half, shift).wait_send()
+
+
+def hand_over(parts, source, target, sem):
+    size = source.shape[1] // parts
+    copies = []
+    for part in range(parts):
+        rows = pl.ds(part * size, size)
+        copies.append(
+            pltpu.make_async_copy(source.at[:, rows], target.at[:, rows], sem.at[part])
+        )
+        copies[-1].start()
+    for copy in copies:
+        copy.wait()
 
 
 def on_device_fused(
@@ -504,15 +550,16 @@
         functools.partial(fused_kernel, blocks),
         out_shape=jax.ShapeDtypeStruct((frames_here, width, positions), bf16),
         in_specs=[pl.BlockSpec(memory_space=pltpu.HBM)] * len(args),
-        out_specs=pl.BlockSpec(memory_space=pltpu.VMEM),
-        scratch_shapes=[pltpu.SMEM(a.shape, a.dtype) for a in args[:2]]
+        out_specs=pl.BlockSpec(memory_space=pltpu.HBM),
+        scratch_shapes=[pltpu.VMEM((frames_here, width, positions), bf16), dma((halves, frames_here))]
+        + [pltpu.SMEM(a.shape, a.dtype) for a in args[:2]]
         + [pltpu.VMEM(a.shape, a.dtype) for a in args[2:]]
         + [
             dma((len(args),)),
             pltpu.VMEM((blocks, ref_rows, width), bf16),
-            pltpu.VMEM((halves, frames_here, HEADS, 256, count), bf16),
+            pltpu.VMEM((halves, frames_here, HEADS // 2, 256, 2 * count), bf16),
             pltpu.VMEM((frames_here, 2 * positions, width), bf16),
-            pltpu.VMEM((frames_here, HEADS, width // HEADS, 2 * positions), bf16),
+            pltpu.VMEM((frames_here, HEADS // 2, 2 * width // HEADS, 2 * positions), bf16),
             pltpu.VMEM((halves, frames_here, width, count), jnp.float32),
             pltpu.VMEM((frames_here, width, count), jnp.float32),
             pltpu.VMEM((width, count), jnp.float32),
@@ -531,6 +578,15 @@
             collective_id=0, has_side_effects=True, vmem_limit_bytes=60 * 1024 * 1024
         ),
     )(*args)
+    parts = 4
+    out = pl.pallas_call(
+        functools.partial(hand_over, parts),
+        out_shape=jax.ShapeDtypeStruct(out.shape, out.dtype),
+        in_specs=[pl.BlockSpec(memory_space=pltpu.HBM)],
+        out_specs=pl.BlockSpec(memory_space=pltpu.HBM),
+        scratch_shapes=[dma((parts,))],
+        compiler_params=pltpu.CompilerParams(vmem_limit_bytes=60 * 1024 * 1024),
+    )(out)
     return out.transpose(0, 2, 1)
 
 

time: 38 us -> 47.4 us (1.25)
  Pallas kernels: 35.4 us -> 46.6 us
  local copies, waits for them, and re-layouts: 1.72 us -> 0 us
    pallas_call x0 -> x1, Pallas kernels: none -> 11.1 us  [on_device_fused(): pl.pallas_call(functools.partial(hand_over, parts), out_shape=jax.ShapeDt...]
    unnamed x1 -> x0, local copies, waits for them, and re-layouts: 1.72 us -> none
where the time goes in v5:
time: 47.4 us; the launch traced here: 47.3 us
  Pallas kernels  46.6 us (98%)
  between operations  0.66 us (1%)
    pallas_call x1, Pallas kernels, on_device_fused(): pl.pallas_call(functools.partial(fused_kernel, blocks), out_shape=jax.Sha...  35.5 us
    pallas_call x1, Pallas kernels, on_device_fused(): pl.pallas_call(functools.partial(hand_over, parts), out_shape=jax.ShapeDt...  11.1 us

profile of v5, /device:TPU:0, one launch (start us, length us, event | category | flops | bytes accessed | tf_op | source)
XLA Modules:
  0.0 47.3 jit_solution(4030546412594420489)
XLA Ops:
  0.7 35.5 %shard_map.145.source = bf16[2,320,256]{2,1,0:T(8,128)(2,1)} custom-call(s32[1]{0:T(128)S(6)} %copy.16.step_hbm, s32[2]{0:T(128)} %frame_hbm.1, bf16[2,320,256]{2,1,0:T(8,128)(2,1)} %bitcast.4, bf16[32,320]{1,0:T(8,128)(2,1)} %ref_hbm.1, bf16[320,1000]{1,0:T(8,128)(2,1)} %bitcast.3, f32[320]{0:T(512)} %gain1_hbm.1, f32[320]{0:T(512)} %gain2_hbm.1, ...), custom_call_target="tpu_custom_call" | custom-call | tf_op jit(solution)/shard_map/pallas_call | solution.py:549
  36.2 11.1 %shard_map.146 = bf16[2,320,256]{2,1,0:T(8,128)(2,1)} custom-call(bf16[2,320,256]{2,1,0:T(8,128)(2,1)} %shard_map.145.source), custom_call_target="tpu_custom_call" | custom-call | tf_op jit(solution)/shard_map/pallas_call | solution.py:582

commit v6 on v5

--- a/solution.py
+++ b/solution.py
@@ -137,48 +137,6 @@
     low = head * head_dim
     high = low + head_dim
     return low, high, low // 128 * 128, min(width, -(-high // 128) * 128)
-
-
-def lane_mask(low, high, first, last):
-    lane = lax.broadcasted_iota(jnp.int32, (1, last - first), 1) + first
-    return jnp.where((lane >= low) & (lane < high), 1.0, 0.0).astype(jnp.bfloat16)
-
-
-def attend_heads(q, key_parts, value_parts, width, allowed=None):
-    head_dim = width // HEADS
-    factor = math.log2(math.e) / math.sqrt(head_dim)
-    columns = [None] * (-(-width // 128))
-    for head in range(HEADS):
-        low, high, first, last = head_span(head, head_dim, width)
-        picked = q[:, first:last] * lane_mask(low, high, first, last)
-        scores = [
-            lax.dot_general(
-                picked,
-                keys(first, last),
-                (((1,), (1,)), ((), ())),
-                preferred_element_type=jnp.float32,
-            )
-            for keys in key_parts
-        ]
-        if allowed is not None:
-            scores = [jnp.where(allowed, s, -1e30) for s in scores]
-        top = functools.reduce(jnp.maximum, [jnp.max(s, axis=-1, keepdims=True) for s in scores])
-        exps = [jnp.exp2((s - top) * factor) for s in scores]
-        total = sum(jnp.sum(e, axis=-1, keepdims=True) for e in exps)
-        inverse = 1.0 / total
-        result = None
-        for e, values in zip(exps, value_parts):
-            probs = (e * inverse).astype(jnp.bfloat16)
-            part = jnp.dot(probs, values(first, last), preferred_element_type=jnp.float32)
-            result = part if result is None else result + part
-        for block in range(first // 128, -(-last // 128)):
-            start, end = block * 128, min(width, block * 128 + 128)
-            piece = result[:, start - first : end - first]
-            if columns[block] is not None:
-                lane = lax.broadcasted_iota(jnp.int32, (1, end - start), 1) + start
-                piece = jnp.where(lane >= low, piece, columns[block])
-            columns[block] = piece
-    return jnp.concatenate(columns, axis=-1)
 
 
 def fused_kernel(
@@ -220,6 +178,7 @@
     ref_buf,
     q_buf,
     k_buf,
+    self_buf,
     v_buf,
     mid_buf,
     pe_buf,
@@ -329,7 +288,7 @@
     def column(row):
         return jnp.broadcast_to(row, (count, width)).T
 
-    for load in loads[2:]:
+    for load in loads[2:9]:
         load.wait()
     steps = temb_ref.shape[1]
     chosen = lax.broadcasted_iota(jnp.int32, (steps, count), 0) == step_ref[0]
@@ -361,10 +320,11 @@
         return jnp.concatenate([one, two], axis=1).astype(bf16)
 
     def weigh(scores):
-        top = jnp.max(scores, axis=0, keepdims=True)
-        exps = jnp.exp2((scores - top) * factor)
-        inverse = 1.0 / jnp.sum(exps, axis=0, keepdims=True)
-        return (exps * inverse).astype(bf16)
+        tops = [jnp.max(s, axis=0, keepdims=True) for s in scores]
+        top = functools.reduce(jnp.maximum, tops)
+        exps = [jnp.exp2((s - top) * factor) for s in scores]
+        inverse = 1.0 / sum(jnp.sum(e, axis=0, keepdims=True) for e in exps)
+        return jnp.concatenate([(e * inverse).astype(bf16) for e in exps], axis=0)
 
     def own_rows(values, probs):
         both = jnp.dot(values, probs, preferred_element_type=jnp.float32)
@@ -380,32 +340,36 @@
             normed.append(layer_norm_down(base, gain1).astype(bf16))
         normed = jnp.concatenate(normed, axis=1)
         query = project_down(spq_ref[...], normed, 0)
+        key = project(normed.T, spk_ref[...])
         for half in range(halves):
             for pair in range(HEADS // 2):
                 first, last = pair_span(pair)
-                piece = query[first:last, half * count : (half + 1) * count]
-                q_buf[half, f, pair, : last - first] = by_head(pair, piece)
-        k_buf[f, :positions] = project(normed.T, spk_ref[...])
+                picked = by_head(pair, query[first:last, half * count : (half + 1) * count])
+                q_buf[half, f, pair, : last - first] = picked
+                self_buf[half, f, pair] = jnp.dot(
+                    key[:, first:last], picked, preferred_element_type=jnp.float32
+                )
         value = project_down(spv_ref[...], normed, 0)
         v_buf[f, :, :, :positions] = value.reshape(pair_shape).astype(bf16)
 
+    for load in loads[9:11]:
+        load.wait()
+    gain2_buf[...] = column(gain2_ref[...].reshape(1, width))
     for shift in range(1, blocks):
         ref_copy(shift).wait_recv()
     ref_all = ref_buf[...].reshape(-1, width)
-    ref_key = project(ref_all, spk_ref[...])
+    k_buf[...] = project(ref_all, spk_ref[...])
     ref_value = project_down(spv_ref[...], ref_all, 1)
     ref_value = ref_value.reshape(pair_shape).astype(bf16)
     for f in range(frames_here):
-        k_buf[f, positions:] = ref_key
         v_buf[f, :, :, positions:] = ref_value
 
-    gain2_buf[...] = column(gain2_ref[...].reshape(1, width))
 
     def spatial(half, carry):
         def score(f, pair):
             first, last = pair_span(pair)
             return jnp.dot(
-                k_buf[f, :, first:last],
+                k_buf[:, first:last],
                 q_buf[half, f, pair, : last - first],
                 preferred_element_type=jnp.float32,
             )
@@ -419,7 +383,7 @@
                 place = units.index((f, pair)) + 1
                 if place < len(units):
                     ahead = score(*units[place])
-                done += own_rows(v_buf[f, pair], weigh(scores))
+                done += own_rows(v_buf[f, pair], weigh([self_buf[half, f, pair], scores]))
             attn = jnp.concatenate(done, axis=0).astype(bf16)
             mid = mid_buf[half, f] + project_down(spo_ref[...], attn, 0)
             mid_buf[half, f] = mid
@@ -439,33 +403,43 @@
 
     lax.fori_loop(0, halves, spatial, 0)
 
+    for load in loads[11:]:
+        load.wait()
     group = 8
-    size = frames * group
-    row_pos = lax.broadcasted_iota(jnp.int32, (size, size), 0) % group
-    col_pos = lax.broadcasted_iota(jnp.int32, (size, size), 1) % group
+    row_pos = lax.broadcasted_iota(jnp.int32, (count, 2 * count), 0) % group
+    col_pos = lax.broadcasted_iota(jnp.int32, (count, 2 * count), 1) % group
     same = row_pos == col_pos
 
     def temporal(half, carry):
         for shift in range(1, blocks):
             for f in range(frames_here):
                 fwd_copy(half, f, shift).wait_recv()
-        normed = jnp.concatenate(unpack(fwd_in[half]), axis=0).reshape(frames * rows, width)
-
-        def grouped(weight_ref):
-            full = jnp.dot(normed, weight_ref[...], preferred_element_type=jnp.float32)
-            full = full.reshape(frames, rows // group, group, width)
-            return [full[:, g].reshape(size, width).astype(bf16) for g in range(rows // group)]
-
-        q2, k2, v2 = grouped(tmq_ref), grouped(tmk_ref), grouped(tmv_ref)
+        normed = jnp.concatenate(unpack(fwd_in[half]), axis=0).astype(jnp.float32)
+        normed = normed.reshape(frames, rows // group, group, width)
+        normed = jnp.concatenate(
+            [normed[:, g].reshape(count, width) for g in range(rows // group)], axis=0
+        ).astype(bf16)
+        query = project_down(tmq_ref[...], normed, 1)
+        key = project(normed, tmk_ref[...])
+        value = project_down(tmv_ref[...], normed, 1).reshape(HEADS // 2, 2 * head_dim, -1)
+        value = value.astype(bf16)
+
+        def score(g, pair):
+            first, last = pair_span(pair)
+            columns = slice(g * count, (g + 1) * count)
+            picked = by_head(pair, query[first:last, columns])
+            found = jnp.dot(
+                key[columns, first:last], picked, preferred_element_type=jnp.float32
+            )
+            return jnp.where(same, found, -1e30)
+
         done = []
         for g in range(rows // group):
-            attn = attend_heads(
-                q2[g],
-                [lambda a, b: k2[g][:, a:b]],
-                [lambda a, b: v2[g][:, a:b]],
-                width,
-                same,
-            )
+            attn = []
+            for pair in range(HEADS // 2):
+                probs = weigh([score(g, pair)])
+                attn += own_rows(value[pair, :, g * count : (g + 1) * count], probs)
+            attn = jnp.concatenate(attn, axis=0).T
             done.append(attn.reshape(frames, 1, group, width))
         attn = jnp.concatenate(done, axis=1).reshape(frames, rows, width).astype(bf16)
         bwd_out[half] = pack(attn[:blocks], attn[blocks:])
@@ -501,19 +475,6 @@
             for f in range(frames_here):
                 fwd_copy(half, f, shift).wait_send()
             bwd_copy(half, shift).wait_send()
-
-
-def hand_over(parts, source, target, sem):
-    size = source.shape[1] // parts
-    copies = []
-    for part in range(parts):
-        rows = pl.ds(part * size, size)
-        copies.append(
-            pltpu.make_async_copy(source.at[:, rows], target.at[:, rows], sem.at[part])
-        )
-        copies[-1].start()
-    for copy in copies:
-        copy.wait()
 
 
 def on_device_fused(
@@ -558,7 +519,8 @@
             dma((len(args),)),
             pltpu.VMEM((blocks, ref_rows, width), bf16),
             pltpu.VMEM((halves, frames_here, HEADS // 2, 256, 2 * count), bf16),
-            pltpu.VMEM((frames_here, 2 * positions, width), bf16),
+            pltpu.VMEM((blocks * ref_rows, width), bf16),
+            pltpu.VMEM((halves, frames_here, HEADS // 2, positions, 2 * count), jnp.float32),
             pltpu.VMEM((frames_here, HEADS // 2, 2 * width // HEADS, 2 * positions), bf16),
             pltpu.VMEM((halves, frames_here, width, count), jnp.float32),
             pltpu.VMEM((frames_here, width, count), jnp.float32),
@@ -578,15 +540,6 @@
             collective_id=0, has_side_effects=True, vmem_limit_bytes=60 * 1024 * 1024
         ),
     )(*args)
-    parts = 4
-    out = pl.pallas_call(
-        functools.partial(hand_over, parts),
-        out_shape=jax.ShapeDtypeStruct(out.shape, out.dtype),
-        in_specs=[pl.BlockSpec(memory_space=pltpu.HBM)],
-        out_specs=pl.BlockSpec(memory_space=pltpu.HBM),
-        scratch_shapes=[dma((parts,))],
-        compiler_params=pltpu.CompilerParams(vmem_limit_bytes=60 * 1024 * 1024),
-    )(out)
     return out.transpose(0, 2, 1)
 
 
@@ -600,7 +553,7 @@
         and 2 * width % 128 == 0
         and blocks * ref_feats.shape[0] == positions
         and ref_feats.shape[0] % 16 == 0
-        and frames_here * blocks * 8 <= 128
+        and frames_here * blocks * 8 == positions // 2
     )
     body = on_device_fused if fits else on_device_plain
     return body(hidden, ref_feats, frame_index, step_index, temb_table, *rest)

time: 47.4 us -> 34.5 us (0.73)
  Pallas kernels: 46.6 us -> 32 us
  local copies, waits for them, and re-layouts: 0 us -> 1.72 us
    pallas_call x1 -> x0, Pallas kernels: 11.1 us -> none  [on_device_fused(): pl.pallas_call(functools.partial(hand_over, parts), out_shape=jax.ShapeDt...]
    pallas_call x1, Pallas kernels: 35.5 us -> 32 us  [on_device_fused(): pl.pallas_call(functools.partial(fused_kernel, blocks), out_shape=jax.Sha...]
    unnamed x0 -> x1, local copies, waits for them, and re-layouts: none -> 1.72 us
where the time goes in v6:
time: 34.5 us; the launch traced here: 34.4 us
  Pallas kernels  32 us (93%)
  local copies, waits for them, and re-layouts  1.72 us (5%)
  between operations  0.66 us (2%)
    pallas_call x1, Pallas kernels, on_device_fused(): pl.pallas_call(functools.partial(fused_kernel, blocks), out_shape=jax.Sha...  32 us
    unnamed x1, local copies, waits for them, and re-layouts  1.72 us

profile of v6, /device:TPU:0, one launch (start us, length us, event | category | flops | bytes accessed | tf_op | source)
XLA Modules:
  0.0 34.4 jit_solution(14025819664837867747)
XLA Ops:
  0.7 32.0 %shard_map.145 = bf16[2,320,256]{2,1,0:T(8,128)(2,1)} custom-call(s32[1]{0:T(128)S(6)} %copy.17.step_hbm, s32[2]{0:T(128)} %frame_hbm.1, bf16[2,320,256]{2,1,0:T(8,128)(2,1)} %bitcast.5, bf16[32,320]{1,0:T(8,128)(2,1)} %ref_hbm.1, bf16[320,1000]{1,0:T(8,128)(2,1)} %bitcast.4, f32[320]{0:T(512)} %gain1_hbm.1, f32[320]{0:T(512)} %gain2_hbm.1, ...), custom_call_target="tpu_custom_call" | custom-call | tf_op jit(solution)/shard_map/pallas_call | solution.py:510
  32.7 1.7 %copy.18 = bf16[2,256,320]{1,2,0:T(8,128)(2,1)} copy(bf16[2,256,320]{1,2,0:T(8,128)(2,1)} %bitcast.3) | data formatting | bytes 655360

commit v7 on v6

--- a/solution.py
+++ b/solution.py
@@ -139,6 +139,44 @@
     return low, high, low // 128 * 128, min(width, -(-high // 128) * 128)
 
 
+def unpack(both, width):
+    split = 2 * width - width // 128 * 128
+    return both[..., :width], jnp.concatenate([both[..., split:], both[..., width:split]], axis=-1)
+
+
+def finish_kernel(attn_hbm, mid_hbm, tmo_hbm, out_hbm, attn_ref, mid_ref, tmo_ref, out_ref, load_sem, store_sem):
+    halves, frames_here, width, count = mid_ref.shape
+    weight = pltpu.make_async_copy(tmo_hbm, tmo_ref, load_sem.at[halves, 0])
+    weight.start()
+    loads = []
+    for half in range(halves):
+        pair = (
+            pltpu.make_async_copy(attn_hbm.at[half], attn_ref.at[half], load_sem.at[half, 0]),
+            pltpu.make_async_copy(mid_hbm.at[half], mid_ref.at[half], load_sem.at[half, 1]),
+        )
+        for load in pair:
+            load.start()
+        loads.append(pair)
+    weight.wait()
+    stores = []
+    for half in range(halves):
+        for load in loads[half]:
+            load.wait()
+        columns = pl.ds(half * count, count)
+        for f, attn in enumerate(unpack(attn_ref[half], width)):
+            attn = attn.reshape(count, width)
+            mixed = mid_ref[half, f] + project_down(tmo_ref[...], attn, 1)
+            out_ref[f, :, half * count : (half + 1) * count] = mixed.astype(jnp.bfloat16)
+            stores.append(
+                pltpu.make_async_copy(
+                    out_ref.at[f, :, columns], out_hbm.at[f, :, columns], store_sem.at[half, f]
+                )
+            )
+            stores[-1].start()
+    for store in stores:
+        store.wait()
+
+
 def fused_kernel(
     blocks,
     step_hbm,
@@ -155,10 +193,10 @@
     tmq_hbm,
     tmk_hbm,
     tmv_hbm,
-    tmo_hbm,
-    out_hbm,
-    out_ref,
-    store_sem,
+    attn_hbm,
+    mid_hbm,
+    own_sem,
+    mid_sem,
     step_ref,
     frame_ref,
     hidden_ref,
@@ -173,12 +211,13 @@
     tmq_ref,
     tmk_ref,
     tmv_ref,
-    tmo_ref,
     load_sem,
     ref_buf,
     q_buf,
     k_buf,
     self_buf,
+    top_buf,
+    sum_buf,
     v_buf,
     mid_buf,
     pe_buf,
@@ -186,7 +225,6 @@
     fwd_out,
     fwd_in,
     bwd_out,
-    bwd_in,
     ref_send,
     ref_recv,
     fwd_send,
@@ -223,7 +261,6 @@
                 (tmq_hbm, tmq_ref),
                 (tmk_hbm, tmk_ref),
                 (tmv_hbm, tmv_ref),
-                (tmo_hbm, tmo_ref),
             )
         )
     ]
@@ -265,17 +302,23 @@
             device_id_type=pl.DeviceIdType.MESH,
         )
 
+    def own_copy(half):
+        return pltpu.make_async_copy(
+            bwd_out.at[half, me], attn_hbm.at[half, me], own_sem.at[half]
+        )
+
+    def mid_copy(half, f):
+        return pltpu.make_async_copy(
+            mid_buf.at[half, f], mid_hbm.at[half, f], mid_sem.at[half, f]
+        )
+
     def pack(first, second):
         return jnp.concatenate([first, second[..., whole:], second[..., :whole]], axis=-1)
-
-    def unpack(both):
-        second = [both[..., 2 * width - whole :], both[..., width : 2 * width - whole]]
-        return both[..., :width], jnp.concatenate(second, axis=-1)
 
     def bwd_copy(half, shift):
         return pltpu.make_async_remote_copy(
             src_ref=bwd_out.at[half, peer(shift)],
-            dst_ref=bwd_in.at[half, me],
+            dst_ref=attn_hbm.at[half, me],
             send_sem=bwd_send.at[half, shift - 1],
             recv_sem=bwd_recv.at[half, shift - 1],
             device_id={"frame": peer(shift)},
@@ -319,12 +362,10 @@
         two = jnp.where((row >= middle) & (row < end), piece, 0.0)
         return jnp.concatenate([one, two], axis=1).astype(bf16)
 
-    def weigh(scores):
-        tops = [jnp.max(s, axis=0, keepdims=True) for s in scores]
-        top = functools.reduce(jnp.maximum, tops)
-        exps = [jnp.exp2((s - top) * factor) for s in scores]
-        inverse = 1.0 / sum(jnp.sum(e, axis=0, keepdims=True) for e in exps)
-        return jnp.concatenate([(e * inverse).astype(bf16) for e in exps], axis=0)
+    def raised(scores):
+        top = jnp.max(scores, axis=0, keepdims=True)
+        exps = jnp.exp2((scores - top) * factor)
+        return top, exps, jnp.sum(exps, axis=0, keepdims=True)
 
     def own_rows(values, probs):
         both = jnp.dot(values, probs, preferred_element_type=jnp.float32)
@@ -346,9 +387,12 @@
                 first, last = pair_span(pair)
                 picked = by_head(pair, query[first:last, half * count : (half + 1) * count])
                 q_buf[half, f, pair, : last - first] = picked
-                self_buf[half, f, pair] = jnp.dot(
-                    key[:, first:last], picked, preferred_element_type=jnp.float32
+                top, exps, total = raised(
+                    jnp.dot(key[:, first:last], picked, preferred_element_type=jnp.float32)
                 )
+                self_buf[half, f, pair] = exps
+                top_buf[half, f, pair] = top
+                sum_buf[half, f, pair] = total
         value = project_down(spv_ref[...], normed, 0)
         v_buf[f, :, :, :positions] = value.reshape(pair_shape).astype(bf16)
 
@@ -383,10 +427,21 @@
                 place = units.index((f, pair)) + 1
                 if place < len(units):
                     ahead = score(*units[place])
-                done += own_rows(v_buf[f, pair], weigh([self_buf[half, f, pair], scores]))
+                ref_top, exps, total = raised(scores)
+                self_top = top_buf[half, f, pair]
+                top = jnp.maximum(self_top, ref_top)
+                self_part = jnp.exp2((self_top - top) * factor)
+                ref_part = jnp.exp2((ref_top - top) * factor)
+                inverse = 1.0 / (sum_buf[half, f, pair] * self_part + total * ref_part)
+                probs = [
+                    (self_buf[half, f, pair] * (self_part * inverse)).astype(bf16),
+                    (exps * (ref_part * inverse)).astype(bf16),
+                ]
+                done += own_rows(v_buf[f, pair], jnp.concatenate(probs, axis=0))
             attn = jnp.concatenate(done, axis=0).astype(bf16)
             mid = mid_buf[half, f] + project_down(spo_ref[...], attn, 0)
             mid_buf[half, f] = mid
+            mid_copy(half, f).start()
             normed = layer_norm_down(mid, gain2_buf[...]) + pe_buf[f]
             normed = normed.T.astype(bf16).reshape(blocks, rows, width)
             if f == 0:
@@ -414,7 +469,7 @@
         for shift in range(1, blocks):
             for f in range(frames_here):
                 fwd_copy(half, f, shift).wait_recv()
-        normed = jnp.concatenate(unpack(fwd_in[half]), axis=0).astype(jnp.float32)
+        normed = jnp.concatenate(unpack(fwd_in[half], width), axis=0).astype(jnp.float32)
         normed = normed.reshape(frames, rows // group, group, width)
         normed = jnp.concatenate(
             [normed[:, g].reshape(count, width) for g in range(rows // group)], axis=0
@@ -437,7 +492,8 @@
         for g in range(rows // group):
             attn = []
             for pair in range(HEADS // 2):
-                probs = weigh([score(g, pair)])
+                _, exps, total = raised(score(g, pair))
+                probs = (exps * (1.0 / total)).astype(bf16)
                 attn += own_rows(value[pair, :, g * count : (g + 1) * count], probs)
             attn = jnp.concatenate(attn, axis=0).T
             done.append(attn.reshape(frames, 1, group, width))
@@ -445,30 +501,17 @@
         bwd_out[half] = pack(attn[:blocks], attn[blocks:])
         for shift in range(1, blocks):
             bwd_copy(half, shift).start()
-        bwd_in[half, me] = bwd_out[half, me]
+        own_copy(half).start()
         return carry
 
     lax.fori_loop(0, halves, temporal, 0)
 
-    stores = []
     for half in range(halves):
+        own_copy(half).wait()
+        for f in range(frames_here):
+            mid_copy(half, f).wait()
         for shift in range(1, blocks):
             bwd_copy(half, shift).wait_recv()
-        for f, attn in enumerate(unpack(bwd_in[half])):
-            attn = attn.reshape(count, width)
-            mixed = mid_buf[half, f] + project_down(tmo_ref[...], attn, 1)
-            out_ref[f, :, half * count : (half + 1) * count] = mixed.astype(bf16)
-            stores.append(
-                pltpu.make_async_copy(
-                    out_ref.at[f, :, pl.ds(half * count, count)],
-                    out_hbm.at[f, :, pl.ds(half * count, count)],
-                    store_sem.at[half, f],
-                )
-            )
-            stores[-1].start()
-
-    for store in stores:
-        store.wait()
     for shift in range(1, blocks):
         ref_copy(shift).wait_send()
         for half in range(halves):
@@ -504,15 +547,20 @@
         temb_table.T,
         norm_gain_1,
         norm_gain_2,
-        *weights,
-    )
+        *weights[:-1],
+    )
+    hbm = pl.BlockSpec(memory_space=pltpu.HBM)
     moved = (halves, blocks, rows, frames_here * width)
-    out = pl.pallas_call(
+    params = pltpu.CompilerParams(vmem_limit_bytes=60 * 1024 * 1024)
+    attn, mid = pl.pallas_call(
         functools.partial(fused_kernel, blocks),
-        out_shape=jax.ShapeDtypeStruct((frames_here, width, positions), bf16),
-        in_specs=[pl.BlockSpec(memory_space=pltpu.HBM)] * len(args),
-        out_specs=pl.BlockSpec(memory_space=pltpu.HBM),
-        scratch_shapes=[pltpu.VMEM((frames_here, width, positions), bf16), dma((halves, frames_here))]
+        out_shape=(
+            jax.ShapeDtypeStruct(moved, bf16),
+            jax.ShapeDtypeStruct((halves, frames_here, width, count), jnp.float32),
+        ),
+        in_specs=[hbm] * len(args),
+        out_specs=(hbm, hbm),
+        scratch_shapes=[dma((halves,)), dma((halves, frames_here))]
         + [pltpu.SMEM(a.shape, a.dtype) for a in args[:2]]
         + [pltpu.VMEM(a.shape, a.dtype) for a in args[2:]]
         + [
@@ -521,11 +569,12 @@
             pltpu.VMEM((halves, frames_here, HEADS // 2, 256, 2 * count), bf16),
             pltpu.VMEM((blocks * ref_rows, width), bf16),
             pltpu.VMEM((halves, frames_here, HEADS // 2, positions, 2 * count), jnp.float32),
+            pltpu.VMEM((halves, frames_here, HEADS // 2, 1, 2 * count), jnp.float32),
+            pltpu.VMEM((halves, frames_here, HEADS // 2, 1, 2 * count), jnp.float32),
             pltpu.VMEM((frames_here, HEADS // 2, 2 * width // HEADS, 2 * positions), bf16),
             pltpu.VMEM((halves, frames_here, width, count), jnp.float32),
             pltpu.VMEM((frames_here, width, count), jnp.float32),
             pltpu.VMEM((width, count), jnp.float32),
-            pltpu.VMEM(moved, bf16),
             pltpu.VMEM(moved, bf16),
             pltpu.VMEM(moved, bf16),
             pltpu.VMEM(moved, bf16),
@@ -540,6 +589,22 @@
             collective_id=0, has_side_effects=True, vmem_limit_bytes=60 * 1024 * 1024
         ),
     )(*args)
+    out_shape = (frames_here, width, positions)
+    out = pl.pallas_call(
+        finish_kernel,
+        out_shape=jax.ShapeDtypeStruct(out_shape, bf16),
+        in_specs=[hbm] * 3,
+        out_specs=hbm,
+        scratch_shapes=[
+            pltpu.VMEM(moved, bf16),
+            pltpu.VMEM(mid.shape, jnp.float32),
+            pltpu.VMEM(weights[-1].shape, bf16),
+            pltpu.VMEM(out_shape, bf16),
+            dma((halves + 1, 2)),
+            dma((halves, frames_here)),
+        ],
+        compiler_params=params,
+    )(attn, mid, weights[-1])
     return out.transpose(0, 2, 1)
 
 

time: 34.5 us -> 34.3 us (level)
  local copies, waits for them, and re-layouts: 1.72 us -> 0 us
  Pallas kernels: 32 us -> 33.5 us
    unnamed x1 -> x0, local copies, waits for them, and re-layouts: 1.72 us -> none
    pallas_call x1 -> x2, Pallas kernels: 32 us -> 33.5 us  [the longest x1 30.9 us: on_device_fused(): pl.pallas_call(functools.partial(fused_kernel, blocks), out_shape=(jax.Sh...]
where the time goes in v7:
time: 34.3 us; the launch traced here: 34.2 us
  Pallas kernels  33.5 us (98%)
  between operations  0.66 us (2%)
    pallas_call x1, Pallas kernels, on_device_fused(): pl.pallas_call(functools.partial(fused_kernel, blocks), out_shape=(jax.Sh...  30.9 us
    pallas_call x1, Pallas kernels, on_device_fused(): pl.pallas_call(finish_kernel, out_shape=jax.ShapeDtypeStruct(out_shape, b...  2.63 us

profile of v7, /device:TPU:0, one launch (start us, length us, event | category | flops | bytes accessed | tf_op | source)
XLA Modules:
  0.0 34.2 jit_solution(12720684290086548309)
XLA Ops:
  0.7 30.9 %shard_map.145 = (bf16[2,8,16,640]{3,2,1,0:T(8,128)(2,1)}, f32[2,2,320,128]{3,2,1,0:T(8,128)}) custom-call(s32[1]{0:T(128)S(6)} %copy.16.step_hbm, s32[2]{0:T(128)} %frame_hbm.1, bf16[2,320,256]{2,1,0:T(8,128)(2,1)} %bitcast.4, bf16[32,320]{1,0:T(8,128)(2,1)} %ref_hbm.1, bf16[320,1000]{1,0:T(8,128)(2,1)} %bitcast.3, f32[320]{0:T(512)} %gain1_hbm.1, ...), custom_call_target="tpu_custom_call" | custom-call | tf_op jit(solution)/shard_map/pallas_call | solution.py:555
  31.5 2.6 %shard_map.146 = bf16[2,320,256]{2,1,0:T(8,128)(2,1)} custom-call(bf16[2,8,16,640]{3,2,1,0:T(8,128)(2,1)} %get-tuple-element.7.attn_hbm, f32[2,2,320,128]{3,2,1,0:T(8,128)} %get-tuple-element.8.mid_hbm, bf16[320,320]{1,0:T(8,128)(2,1)} %tmo_hbm.1), custom_call_target="tpu_custom_call" | custom-call | tf_op jit(solution)/shard_map/pallas_call | solution.py:593

commit v8 on v7

--- a/solution.py
+++ b/solution.py
@@ -240,6 +240,8 @@
     head_dim = width // HEADS
     bf16 = jnp.bfloat16
 
+    order = sorted(range(1, blocks), key=lambda shift: abs(2 * shift - blocks))
+
     def peer(shift):
         return lax.rem(me + shift, blocks)
 
@@ -325,7 +327,7 @@
             device_id_type=pl.DeviceIdType.MESH,
         )
 
-    for shift in range(1, blocks):
+    for shift in order:
         ref_copy(shift).start()
 
     def column(row):
@@ -451,7 +453,7 @@
                 fwd_out[half, :, :, whole:] = jnp.concatenate(
                     [first_tail, normed[:, :, whole:], normed[:, :, :whole]], axis=-1
                 )
-            for shift in range(1, blocks):
+            for shift in order:
                 fwd_copy(half, f, shift).start()
         fwd_in[half, me] = fwd_out[half, me]
         return carry
@@ -499,7 +501,7 @@
             done.append(attn.reshape(frames, 1, group, width))
         attn = jnp.concatenate(done, axis=1).reshape(frames, rows, width).astype(bf16)
         bwd_out[half] = pack(attn[:blocks], attn[blocks:])
-        for shift in range(1, blocks):
+        for shift in order:
             bwd_copy(half, shift).start()
         own_copy(half).start()
         return carry

time: 34.3 us -> 34.5 us (level)
  no operation moved by 1% of the time
where the time goes in v8:
time: 34.5 us; the launch traced here: 34.4 us
  Pallas kernels  33.7 us (98%)
  between operations  0.66 us (2%)
    pallas_call x1, Pallas kernels, on_device_fused(): pl.pallas_call(functools.partial(fused_kernel, blocks), out_shape=(jax.Sh...  31.1 us
    pallas_call x1, Pallas kernels, on_device_fused(): pl.pallas_call(finish_kernel, out_shape=jax.ShapeDtypeStruct(out_shape, b...  2.63 us

profile of v8, /device:TPU:0, one launch (start us, length us, event | category | flops | bytes accessed | tf_op | source)
XLA Modules:
  0.0 34.4 jit_solution(7190485729792812041)
XLA Ops:
  0.7 31.1 %shard_map.145 = (bf16[2,8,16,640]{3,2,1,0:T(8,128)(2,1)}, f32[2,2,320,128]{3,2,1,0:T(8,128)}) custom-call(s32[1]{0:T(128)S(6)} %copy.16.step_hbm, s32[2]{0:T(128)} %frame_hbm.1, bf16[2,320,256]{2,1,0:T(8,128)(2,1)} %bitcast.4, bf16[32,320]{1,0:T(8,128)(2,1)} %ref_hbm.1, bf16[320,1000]{1,0:T(8,128)(2,1)} %bitcast.3, f32[320]{0:T(512)} %gain1_hbm.1, ...), custom_call_target="tpu_custom_call" | custom-call | tf_op jit(solution)/shard_map/pallas_call | solution.py:557
  31.7 2.6 %shard_map.146 = bf16[2,320,256]{2,1,0:T(8,128)(2,1)} custom-call(bf16[2,8,16,640]{3,2,1,0:T(8,128)(2,1)} %get-tuple-element.7.attn_hbm, f32[2,2,320,128]{3,2,1,0:T(8,128)} %get-tuple-element.8.mid_hbm, bf16[320,320]{1,0:T(8,128)(2,1)} %tmo_hbm.1), custom_call_target="tpu_custom_call" | custom-call | tf_op jit(solution)/shard_map/pallas_call | solution.py:595

commit v9 on v6

--- a/solution.py
+++ b/solution.py
@@ -179,6 +179,8 @@
     q_buf,
     k_buf,
     self_buf,
+    top_buf,
+    sum_buf,
     v_buf,
     mid_buf,
     pe_buf,
@@ -319,12 +321,10 @@
         two = jnp.where((row >= middle) & (row < end), piece, 0.0)
         return jnp.concatenate([one, two], axis=1).astype(bf16)
 
-    def weigh(scores):
-        tops = [jnp.max(s, axis=0, keepdims=True) for s in scores]
-        top = functools.reduce(jnp.maximum, tops)
-        exps = [jnp.exp2((s - top) * factor) for s in scores]
-        inverse = 1.0 / sum(jnp.sum(e, axis=0, keepdims=True) for e in exps)
-        return jnp.concatenate([(e * inverse).astype(bf16) for e in exps], axis=0)
+    def raised(scores):
+        top = jnp.max(scores, axis=0, keepdims=True)
+        exps = jnp.exp2((scores - top) * factor)
+        return top, exps, jnp.sum(exps, axis=0, keepdims=True)
 
     def own_rows(values, probs):
         both = jnp.dot(values, probs, preferred_element_type=jnp.float32)
@@ -346,9 +346,12 @@
                 first, last = pair_span(pair)
                 picked = by_head(pair, query[first:last, half * count : (half + 1) * count])
                 q_buf[half, f, pair, : last - first] = picked
-                self_buf[half, f, pair] = jnp.dot(
-                    key[:, first:last], picked, preferred_element_type=jnp.float32
+                top, exps, total = raised(
+                    jnp.dot(key[:, first:last], picked, preferred_element_type=jnp.float32)
                 )
+                self_buf[half, f, pair] = exps
+                top_buf[half, f, pair] = top
+                sum_buf[half, f, pair] = total
         value = project_down(spv_ref[...], normed, 0)
         v_buf[f, :, :, :positions] = value.reshape(pair_shape).astype(bf16)
 
@@ -383,7 +386,17 @@
                 place = units.index((f, pair)) + 1
                 if place < len(units):
                     ahead = score(*units[place])
-                done += own_rows(v_buf[f, pair], weigh([self_buf[half, f, pair], scores]))
+                ref_top, exps, total = raised(scores)
+                self_top = top_buf[half, f, pair]
+                top = jnp.maximum(self_top, ref_top)
+                self_part = jnp.exp2((self_top - top) * factor)
+                ref_part = jnp.exp2((ref_top - top) * factor)
+                inverse = 1.0 / (sum_buf[half, f, pair] * self_part + total * ref_part)
+                probs = [
+                    (self_buf[half, f, pair] * (self_part * inverse)).astype(bf16),
+                    (exps * (ref_part * inverse)).astype(bf16),
+                ]
+                done += own_rows(v_buf[f, pair], jnp.concatenate(probs, axis=0))
             attn = jnp.concatenate(done, axis=0).astype(bf16)
             mid = mid_buf[half, f] + project_down(spo_ref[...], attn, 0)
             mid_buf[half, f] = mid
@@ -437,7 +450,8 @@
         for g in range(rows // group):
             attn = []
             for pair in range(HEADS // 2):
-                probs = weigh([score(g, pair)])
+                _, exps, total = raised(score(g, pair))
+                probs = (exps * (1.0 / total)).astype(bf16)
                 attn += own_rows(value[pair, :, g * count : (g + 1) * count], probs)
             attn = jnp.concatenate(attn, axis=0).T
             done.append(attn.reshape(frames, 1, group, width))
@@ -521,6 +535,8 @@
             pltpu.VMEM((halves, frames_here, HEADS // 2, 256, 2 * count), bf16),
             pltpu.VMEM((blocks * ref_rows, width), bf16),
             pltpu.VMEM((halves, frames_here, HEADS // 2, positions, 2 * count), jnp.float32),
+            pltpu.VMEM((halves, frames_here, HEADS // 2, 1, 2 * count), jnp.float32),
+            pltpu.VMEM((halves, frames_here, HEADS // 2, 1, 2 * count), jnp.float32),
             pltpu.VMEM((frames_here, HEADS // 2, 2 * width // HEADS, 2 * positions), bf16),
             pltpu.VMEM((halves, frames_here, width, count), jnp.float32),
             pltpu.VMEM((frames_here, width, count), jnp.float32),

time: 34.5 us -> 34.3 us (level)
  no operation moved by 1% of the time
where the time goes in v9:
time: 34.3 us; the launch traced here: 34.1 us
  Pallas kernels  31.8 us (93%)
  local copies, waits for them, and re-layouts  1.72 us (5%)
  between operations  0.66 us (2%)
    pallas_call x1, Pallas kernels, on_device_fused(): pl.pallas_call(functools.partial(fused_kernel, blocks), out_shape=jax.Sha...  31.8 us
    unnamed x1, local copies, waits for them, and re-layouts  1.72 us

profile of v9, /device:TPU:0, one launch (start us, length us, event | category | flops | bytes accessed | tf_op | source)
XLA Modules:
  0.0 34.1 jit_solution(14856059800836449193)
XLA Ops:
  0.7 31.8 %shard_map.145 = bf16[2,320,256]{2,1,0:T(8,128)(2,1)} custom-call(s32[1]{0:T(128)S(6)} %copy.17.step_hbm, s32[2]{0:T(128)} %frame_hbm.1, bf16[2,320,256]{2,1,0:T(8,128)(2,1)} %bitcast.5, bf16[32,320]{1,0:T(8,128)(2,1)} %ref_hbm.1, bf16[320,1000]{1,0:T(8,128)(2,1)} %bitcast.4, f32[320]{0:T(512)} %gain1_hbm.1, f32[320]{0:T(512)} %gain2_hbm.1, ...), custom_call_target="tpu_custom_call" | custom-call | tf_op jit(solution)/shard_map/pallas_call | solution.py:524
  32.4 1.7 %copy.18 = bf16[2,256,320]{1,2,0:T(8,128)(2,1)} copy(bf16[2,256,320]{1,2,0:T(8,128)(2,1)} %bitcast.3) | data formatting | bytes 655360
